TPU v7x, 32 devices: a whole 2x2x4 slice. The times are simulated.
32 devices in a mesh: rows: 8 (over y, x, core), seq: 4 (over z).
Axes of the slice: x: 2, y: 2, z: 4, core: 2. Of those that a mesh axis runs over, the one named last changes fastest.
Arguments:
- resid_in: bfloat16 [96, 256, 768], P('rows', 'seq'), may hold values from -6 to 6
- mask: int32 [96, 256], P('rows', 'seq'), may hold values from 0 to 1, as said below
- steps_row: int32 [96], P('rows'), may hold values from 0 to 999
- cotangent: bfloat16 [96, 256, 768], P('rows', 'seq'), may hold values from -6 to 6
- attn_master: float32 [2359296], P(('rows', 'seq')), may hold values from -1.7320508 to 1.7320508, as said below
- attn_first: float32 [2359296], P(('rows', 'seq')), may hold values from -224 to 224
- attn_second: float32 [2359296], P(('rows', 'seq')), may hold values from 384 to 12288
- mlp_master: float32 [4718592], P(('rows', 'seq')), may hold values from -0.21875 to 0.21875
- mlp_first: float32 [4718592], P(('rows', 'seq')), may hold values from -224 to 224
- mlp_second: float32 [4718592], P(('rows', 'seq')), may hold values from 384 to 12288
- norm_master: float32 [5, 768], replicated, may hold values from -6 to 6, as said below
- norm_first: float32 [5, 768], replicated, may hold values from -224 to 224
- norm_second: float32 [5, 768], replicated, may hold values from 384 to 12288
- time_master: float32 [1000, 768], replicated, may hold values from -6 to 6
- time_first: float32 [1000, 768], replicated, may hold values from -4 to 4
- time_second: float32 [1000, 768], replicated, may hold values from 1 to 12
Outputs:
- resid_out: bfloat16 [96, 256, 768], P('rows', 'seq')
- grad_in: bfloat16 [96, 256, 768], P('rows', 'seq')
- attn_new: float32 [2359296], P(('rows', 'seq'))
- attn_first_new: float32 [2359296], P(('rows', 'seq'))
- attn_second_new: float32 [2359296], P(('rows', 'seq'))
- attn_copy: bfloat16 [2359296], P(('rows', 'seq'))
- mlp_new: float32 [4718592], P(('rows', 'seq'))
- mlp_first_new: float32 [4718592], P(('rows', 'seq'))
- mlp_second_new: float32 [4718592], P(('rows', 'seq'))
- perceptron_half_precision: bfloat16 [4718592], P(('rows', 'seq'))
- norm_new: float32 [5, 768], replicated
- norm_first_new: float32 [5, 768], replicated
- norm_second_new: float32 [5, 768], replicated
- time_new: float32 [1000, 768], replicated
- time_first_new: float32 [1000, 768], replicated
- time_second_new: float32 [1000, 768], replicated
Inputs may be any that keep to these rules, and one draw needn't show every extreme that they name: `mask`: 1 marks an absorbed token; how many are absorbed varies strongly from sequence to sequence. `attn_master`: truncated normal entries. `norm_master`: gains about 1, biases and the absorbed-token vector of both signs.
All inputs are finite; a program needn't handle non-finite values.
Results may differ from a plain program's by a relative error of at most 0.0095.
Values may be sent and summed in bfloat16 or wider, within the bound.
A program may use at most 192 MiB of HBM per device.

v0:
```python
import jax
import jax.numpy as jnp
from jax import lax
from jax.sharding import PartitionSpec as P

HEAD_DIM = 64
FF = 3072
STEP = 10


PRODUCT_EXACTNESS = lax.Precision.HIGHEST
NORM_EPSILON = 1e-05


def layer_norm(stream, gain, bias):
    centre = jnp.mean(stream, axis=-1, keepdims=True)
    centred = stream - centre
    spread = jnp.mean(centred * centred, axis=-1, keepdims=True)
    return centred * lax.rsqrt(spread + NORM_EPSILON) * gain + bias


def split_heads(block):
    return block.reshape(block.shape[0], block.shape[1] // HEAD_DIM, HEAD_DIM)


def attend_block(pieces):
    query_rows, key_rows, value_rows = pieces
    query_split = split_heads(query_rows)
    key_split = split_heads(key_rows)
    value_split = split_heads(value_rows)
    scores = jnp.einsum(
        "qhe,khe->hqk", query_split, key_split, preferred_element_type=jnp.float32
    ) * HEAD_DIM ** (-0.5)
    soft_weights = jax.nn.softmax(scores, axis=-1)
    attention_result = jnp.einsum(
        "hqk,khe->qhe",
        soft_weights.astype(jnp.bfloat16),
        value_split,
        preferred_element_type=jnp.float32,
    )
    return attention_result.astype(jnp.bfloat16).reshape(query_rows.shape[0], query_rows.shape[1])


def attend_whole(query_rows, key_rows, value_rows):
    return lax.map(attend_block, (query_rows, key_rows, value_rows))


def backward_block(pieces):
    query_rows, key_rows, value_rows, grad_rows = pieces
    query_split = split_heads(query_rows)
    key_split = split_heads(key_rows)
    value_split = split_heads(value_rows)
    grad_split = split_heads(grad_rows)
    scores = jnp.einsum(
        "qhe,khe->hqk", query_split, key_split, preferred_element_type=jnp.float32
    ) * HEAD_DIM ** (-0.5)
    soft_weights, soft_pull = jax.vjp(lambda score_in: jax.nn.softmax(score_in, axis=-1), scores)
    weights_rounded = soft_weights.astype(jnp.bfloat16)
    grad_soft = jnp.einsum(
        "qhe,khe->hqk", grad_split, value_split, preferred_element_type=jnp.float32
    )
    grad_scores = soft_pull(grad_soft)[0].astype(jnp.bfloat16)
    grad_value = jnp.einsum(
        "hqk,qhe->khe", weights_rounded, grad_split, preferred_element_type=jnp.float32
    )
    grad_query = jnp.einsum(
        "hqk,khe->qhe", grad_scores, key_split, preferred_element_type=jnp.float32
    ) * HEAD_DIM ** (-0.5)
    grad_key = jnp.einsum(
        "hqk,qhe->khe", grad_scores, query_split, preferred_element_type=jnp.float32
    ) * HEAD_DIM ** (-0.5)
    row_shape = query_rows.shape
    return (
        grad_query.astype(jnp.bfloat16).reshape(row_shape),
        grad_key.astype(jnp.bfloat16).reshape(row_shape),
        grad_value.astype(jnp.bfloat16).reshape(row_shape),
    )


def forward(
    resid_in,
    mask_float,
    time_rows,
    norm_master,
    hidden_weight_table,
    expansion_weight_table,
    up_matrix,
    down_matrix,
    attend_fn,
):
    model_width = resid_in.shape[2]
    stream_in = (
        resid_in.astype(jnp.float32)
        + mask_float[..., None] * norm_master[4]
        + time_rows[:, None, :]
    )
    first_normalized = layer_norm(stream_in, norm_master[0], norm_master[1]).astype(jnp.bfloat16)
    projection_rows = jnp.einsum(
        "frm,mk->frk", first_normalized, hidden_weight_table, preferred_element_type=jnp.float32
    ).astype(jnp.bfloat16)
    query_rows = projection_rows[..., :model_width]
    key_rows = projection_rows[..., model_width : 2 * model_width]
    value_rows = projection_rows[..., 2 * model_width :]
    attention_result = attend_fn(query_rows, key_rows, value_rows)
    residual_middle = stream_in + jnp.einsum(
        "frm,mk->frk", attention_result, expansion_weight_table, preferred_element_type=jnp.float32
    )
    second_normalized = layer_norm(residual_middle, norm_master[2], norm_master[3]).astype(
        jnp.bfloat16
    )
    preactivation_rows = jnp.einsum(
        "nqz,za->nqa", second_normalized, up_matrix, preferred_element_type=jnp.float32
    )
    activation_rows = jax.nn.gelu(preactivation_rows, approximate=True).astype(jnp.bfloat16)
    stream_out = residual_middle + jnp.einsum(
        "ozj,ji->ozi", activation_rows, down_matrix, preferred_element_type=jnp.float32
    )
    stored = (
        stream_in,
        first_normalized,
        query_rows,
        key_rows,
        value_rows,
        attention_result,
        residual_middle,
        second_normalized,
        preactivation_rows,
        activation_rows,
    )
    return (stream_out, stored)


def adamw(master, moment_one, moment_two, gradient, step_rate):
    first_new = 0.5 * moment_one + 0.5 * gradient
    second_new = 0.5 * moment_two + 0.5 * gradient * gradient
    correct = 1.0 - 0.5**STEP
    update = first_new / correct / (jnp.sqrt(second_new / correct) + 1e-08)
    return (master - step_rate * (update + 0.1 * master), first_new, second_new)


def local(
    resid_in,
    mask,
    steps_row,
    cotangent,
    attn_master,
    attn_first,
    attn_second,
    mlp_master,
    mlp_first,
    mlp_second,
    norm_master,
    norm_first,
    norm_second,
    time_master,
    time_first,
    time_second,
):
    model_width = resid_in.shape[2]
    attn_full, mlp_full = (
        lax.all_gather(attn_master.astype(jnp.bfloat16), ("rows", "seq"), axis=0, tiled=True),
        lax.all_gather(mlp_master.astype(jnp.bfloat16), ("rows", "seq"), axis=0, tiled=True),
    )
    inner_size = 3 * model_width * model_width
    hidden_weight_table = attn_full[:inner_size].reshape(model_width, 3 * model_width)
    expansion_weight_table = attn_full[inner_size:].reshape(model_width, model_width)
    up_matrix = mlp_full[: model_width * FF].reshape(model_width, FF)
    down_matrix = mlp_full[model_width * FF :].reshape(FF, model_width)
    seq_count = lax.axis_size("seq")
    shard_tally = resid_in.shape[0] // seq_count
    resid_use, cot_use, mask_use = (
        lax.all_to_all(resid_in, "seq", split_axis=0, concat_axis=1, tiled=True),
        lax.all_to_all(cotangent, "seq", split_axis=0, concat_axis=1, tiled=True),
        lax.all_to_all(mask.astype(jnp.bfloat16), "seq", split_axis=0, concat_axis=1, tiled=True),
    )
    steps_use = lax.dynamic_slice_in_dim(
        steps_row, lax.axis_index("seq") * shard_tally, shard_tally, 0
    )
    mask_float = mask_use.astype(jnp.float32)
    chooser = (
        steps_use[:, None] == jnp.arange(time_master.shape[0], dtype=jnp.int32)[None, :]
    ).astype(jnp.float32)
    time_rows = jnp.dot(chooser, time_master, precision=PRODUCT_EXACTNESS)
    stream_out, ignored = forward(
        resid_use,
        mask_float,
        time_rows,
        norm_master,
        hidden_weight_table,
        expansion_weight_table,
        up_matrix,
        down_matrix,
        attend_whole,
    )
    barred = lax.optimization_barrier(
        (
            resid_use,
            time_rows,
            norm_master,
            hidden_weight_table,
            expansion_weight_table,
            up_matrix,
            down_matrix,
            stream_out,
        )
    )
    ignored, stored = forward(
        barred[0],
        mask_float,
        barred[1],
        barred[2],
        barred[3],
        barred[4],
        barred[5],
        barred[6],
        attend_whole,
    )
    (
        stream_in,
        first_normalized,
        query_rows,
        key_rows,
        value_rows,
        attention_result,
        residual_middle,
        second_normalized,
        preactivation_rows,
        activation_rows,
    ) = stored
    resid_out = stream_out.astype(jnp.bfloat16)
    grad_out = cot_use.astype(jnp.float32) * mask_float[..., None]
    reduced_gradient = grad_out.astype(jnp.bfloat16)
    down_gradient = jnp.einsum(
        "imn,imk->nk", activation_rows, reduced_gradient, preferred_element_type=jnp.float32
    )
    activation_gradient = jnp.einsum(
        "xno,po->xnp", reduced_gradient, down_matrix, preferred_element_type=jnp.float32
    )
    ignored, gelu_pull = jax.vjp(
        lambda value_in: jax.nn.gelu(value_in, approximate=True), preactivation_rows
    )
    preactivation_gradient = gelu_pull(activation_gradient)[0].astype(jnp.bfloat16)
    up_gradient = jnp.einsum(
        "rag,ray->gy", second_normalized, preactivation_gradient, preferred_element_type=jnp.float32
    )
    perceptron_vector = jnp.concatenate((up_gradient.reshape(-1), down_gradient.reshape(-1)))
    grad_normed_two = jnp.einsum(
        "kuj,xj->kux", preactivation_gradient, up_matrix, preferred_element_type=jnp.float32
    )
    ignored, second_pull = jax.vjp(layer_norm, residual_middle, norm_master[2], norm_master[3])
    back_mid, gain_two, bias_two = second_pull(grad_normed_two)
    grad_mid = grad_out + back_mid
    sublayer_cotangent_sum = grad_mid.astype(jnp.bfloat16)
    grad_outer = jnp.einsum(
        "qik,qij->kj", attention_result, sublayer_cotangent_sum, preferred_element_type=jnp.float32
    )
    grad_attended = jnp.einsum(
        "xdf,qf->xdq",
        sublayer_cotangent_sum,
        expansion_weight_table,
        preferred_element_type=jnp.float32,
    ).astype(jnp.bfloat16)
    grad_query, grad_key, grad_value = lax.map(
        backward_block, (query_rows, key_rows, value_rows, grad_attended)
    )
    mapping_cotangent = jnp.concatenate((grad_query, grad_key, grad_value), axis=2)
    grad_inner = jnp.einsum(
        "qik,qij->kj", first_normalized, mapping_cotangent, preferred_element_type=jnp.float32
    )
    grad_normed_one = jnp.einsum(
        "xdf,qf->xdq", mapping_cotangent, hidden_weight_table, preferred_element_type=jnp.float32
    )
    ignored, first_pull = jax.vjp(layer_norm, stream_in, norm_master[0], norm_master[1])
    back_in, gain_one, bias_one = first_pull(grad_normed_one)
    grad_stream = grad_mid + back_in
    grad_in = grad_stream.astype(jnp.bfloat16)
    grad_absorbed = jnp.sum(mask_float[..., None] * grad_stream, axis=(0, 1))
    time_local = jnp.dot(chooser.T, jnp.sum(grad_stream, axis=1), precision=PRODUCT_EXACTNESS)
    norm_local = jnp.stack((gain_one, bias_one, gain_two, bias_two, grad_absorbed))
    attn_flat = jnp.concatenate((grad_inner.reshape(-1), grad_outer.reshape(-1)))
    attn_shard, mlp_shard = (
        lax.psum_scatter(attn_flat, ("rows", "seq"), scatter_dimension=0, tiled=True),
        lax.psum_scatter(perceptron_vector, ("rows", "seq"), scatter_dimension=0, tiled=True),
    )
    norm_grad, time_grad = lax.psum((norm_local, time_local), ("rows", "seq"))
    resid_out, grad_in = (
        lax.all_to_all(resid_out, "seq", split_axis=1, concat_axis=0, tiled=True),
        lax.all_to_all(grad_in, "seq", split_axis=1, concat_axis=0, tiled=True),
    )
    attn_new, attn_first_new, attn_second_new = adamw(
        attn_master, attn_first, attn_second, attn_shard, 0.05
    )
    mlp_new, mlp_first_new, mlp_second_new = adamw(
        mlp_master, mlp_first, mlp_second, mlp_shard, 0.03
    )
    norm_new, norm_first_new, norm_second_new = adamw(
        norm_master, norm_first, norm_second, norm_grad, 0.2
    )
    time_new, time_first_new, time_second_new = adamw(
        time_master, time_first, time_second, time_grad, 0.3
    )
    return (
        resid_out,
        grad_in,
        attn_new,
        attn_first_new,
        attn_second_new,
        attn_new.astype(jnp.bfloat16),
        mlp_new,
        mlp_first_new,
        mlp_second_new,
        mlp_new.astype(jnp.bfloat16),
        norm_new,
        norm_first_new,
        norm_second_new,
        time_new,
        time_first_new,
        time_second_new,
    )


def solution(mesh):
    return jax.shard_map(
        local,
        mesh=mesh,
        in_specs=(
            P("rows", "seq", None),
            P("rows", "seq"),
            P("rows"),
            P("rows", "seq", None),
            P(("rows", "seq")),
            P(("rows", "seq")),
            P(("rows", "seq")),
            P(("rows", "seq")),
            P(("rows", "seq")),
            P(("rows", "seq")),
            P(),
            P(),
            P(),
            P(),
            P(),
            P(),
        ),
        out_specs=(
            P("rows", "seq", None),
            P("rows", "seq", None),
            P(("rows", "seq")),
            P(("rows", "seq")),
            P(("rows", "seq")),
            P(("rows", "seq")),
            P(("rows", "seq")),
            P(("rows", "seq")),
            P(("rows", "seq")),
            P(("rows", "seq")),
            P(),
            P(),
            P(),
            P(),
            P(),
            P(),
        ),
        check_vma=False,
    )
```

profile of v0, /device:TPU:0, one launch (start us, length us, event | category | flops | bytes accessed | tf_op | source)
XLA Modules:
  0.0 1027.2 jit_solution(17307175928691246215)
XLA Ops:
  11.6 11.7 %all_to_all.76 = bf16[4,3,64]{2,1,0:T(4,128)(2,1)S(1)} all-to-all(bf16[4,3,64]{2,1,0:T(4,128)(2,1)S(1)} %all_to_all.60), channel_id=1, replica_groups=mesh['rows'=8,'seq'=4] {'seq'}, dimensions={0} | all-to-all | bytes 3072 | tf_op jit(solution)/shard_map/all_to_all | solution.py:174
  23.3 38.6 %all_to_all.77 = bf16[12,64,768]{2,1,0:T(8,128)(2,1)S(1)} all-to-all(bf16[12,64,768]{2,1,0:T(8,128)(2,1)S(1)} %copy-done.20), channel_id=1, replica_groups=mesh['rows'=8,'seq'=4] {'seq'}, dimensions={0} | all-to-all | bytes 2359296 | tf_op jit(solution)/shard_map/all_to_all | solution.py:172
  61.9 3.7 all-to-all-start.3
  66.4 3.0 fusion.84
  75.4 28.5 %all-to-all-done.3 = bf16[12,64,768]{2,1,0:T(8,128)(2,1)S(1)} async-done(((bf16[12,64,768]{2,1,0:T(8,128)(2,1)}), bf16[12,64,768]{2,1,0:T(8,128)(2,1)S(1)}, u32[]{:S(2)}, u32[]{:S(2)}) %all-to-all-start.3) | async-done | bytes 1179680 | tf_op jit(solution)/shard_map/all_to_all | solution.py:173
  105.6 3.5 slice.126
  109.1 7.6 reshape.289
  116.7 7.6 slice.106
  129.5 5.6 convolution_convert_fusion.1
  137.9 27.4 %while.34 = (s32[]{:T(128)}, bf16[3,256,768]{1,2,0:T(8,128)(2,1)}, bf16[3,256,768]{2,1,0:T(8,128)(2,1)}, bf16[3,256,768]{2,1,0:T(8,128)(2,1)}, bf16[3,256,768]{2,1,0:T(8,128)(2,1)S(1)}, /*index=5*/s32[]{:T(128)}) while((s32[]{:T(128)}, bf16[3,256,768]{1,2,0:T(8,128)(2,1)}, bf16[3,256,768]{2,1,0:T(8,128)(2,1)}, bf16[3,256,768]{2,1,0:T(8,128)(2,1)}, ...), condition=%wide.region_5.6_spmd, body=%wide.region_2.5_spmd.sunk | while | flops 205455616 | bytes 13394509 | solution.py:45
  139.3 3.5 fusion.182
  148.4 3.4 fusion.182
  153.1 2.3 fusion.183
  157.6 3.5 fusion.182
  165.3 3.0 fusion.112
  170.8 11.1 %all-gather.5.cloned.1.call-done = bf16[4718592]{0:T(1024)(128)(2,1)} async-done(((bf16[147456]{0:T(1024)(128)(2,1)}), bf16[4718592]{0:T(1024)(128)(2,1)}) %all-gather.5.cloned.1.call-update) | async-done | bytes 9437200 | tf_op jit(solution)/shard_map/all_gather | solution.py:162
  181.9 8.2 fusion.109
  190.1 8.2 reshape.291
  198.3 8.2 slice.115
  206.5 9.4 reshape.292
  216.0 14.2 %convolution_add_fusion = bf16[3,256,768]{2,1,0:T(8,128)(2,1)} fusion(f32[3,256,768]{2,1,0:T(8,128)} %copy-done.18, bf16[3072,768,1]{1,0,2:T(8,128)(2,1)} %reshape.292, bf16[768,3072,1]{1,0,2:T(8,128)(2,1)} %reshape.291, f32[768]{0:T(1024)} %get-tuple-element.218, f32[768]{0:T(1024)} %get-tuple-element.217, f32[3,256]{1,0:T(4,128)} %add_rsqrt_fusion.1, ...), kind=kOutput, calls=%fused_computation.118 | convolution fusion | flops 7273119744 | bytes 12988416 | tf_op jit(solution)/shard_map/ozj,ji->ozi/dot_general | solution.py:115
  234.7 3.6 convolution_convert_fusion
  240.3 2.4 copy.133
  242.7 2.4 copy.134
  245.1 2.4 copy.135
  248.5 32.6 %while.35 = (s32[]{:T(128)}, bf16[3,256,768]{1,2,0:T(8,128)(2,1)}, bf16[3,256,768]{1,2,0:T(8,128)(2,1)}, bf16[3,256,768]{1,2,0:T(8,128)(2,1)}, bf16[3,256,768]{1,2,0:T(8,128)(2,1)}, /*index=5*/s32[]{:T(128)}) while((s32[]{:T(128)}, bf16[3,256,768]{1,2,0:T(8,128)(2,1)}, bf16[3,256,768]{1,2,0:T(8,128)(2,1)}, bf16[3,256,768]{1,2,0:T(8,128)(2,1)}, ...), condition=%wide.region_13.14_spmd, body=%wide.region_10.13_spmd.sunk | while | flops 205455616 | bytes 11035213 | solution.py:45
  250.6 4.6 fusion.187
  261.3 4.6 fusion.187
  272.0 4.6 fusion.187
  277.6 2.3 fusion.188
  281.2 3.1 fusion.113
  285.0 6.5 fusion.47
  291.5 10.9 %fusion.38 = bf16[3,256,3072]{2,1,0:T(8,128)(2,1)S(1)} fusion(f32[3,256,3072]{2,1,0:T(8,128)} %fusion.47, bf16[3,256,768]{2,1,0:T(8,128)(2,1)S(1)} %copy-done.25, bf16[3072,768,1]{1,0,2:T(8,128)(2,1)S(1)} %bitcast.222), kind=kOutput, calls=%fused_computation.62 | convolution fusion | flops 3671064576 | bytes 20054016 | tf_op jit(solution)/shard_map/xno,po->xnp/dot_general | solution.py:236
  302.4 12.7 %convolution_bitcast_fusion.1 = f32[3072,768]{1,0:T(8,128)} fusion(bf16[3,256,768]{2,1,0:T(8,128)(2,1)S(1)} %copy-done.25, f32[3,256,3072]{2,1,0:T(8,128)} %fusion.47), kind=kOutput, calls=%fused_computation.74 | convolution fusion | flops 3645112320 | bytes 20054016 | tf_op jit(solution)/shard_map/imn,imk->nk/dot_general | solution.py:233
  315.1 7.1 convolution_bitcast_fusion.2
  322.3 4.8 multiply_reduce_fusion.5
  332.2 3.8 convolution_bitcast_fusion.3
  336.0 59.6 %while.36 = (s32[]{:T(128)}, bf16[3,256,768]{2,1,0:T(8,128)(2,1)}, bf16[3,256,768]{2,1,0:T(8,128)(2,1)}, bf16[3,256,768]{2,1,0:T(8,128)(2,1)}, bf16[3,256,768]{1...) while((s32[]{:T(128)}, bf16[3,256,768]{2,1,0:T(8,128)(2,1)}, ...), condition=%wide.region_22.23_spmd, body=%wide.region_18.22_spmd.sunk | while | flops 513743104 | bytes 53601500 | solution.py:263
  347.7 2.5 multiply_convert_fusion.4
  350.9 2.5 fusion.200
  367.5 2.5 multiply_convert_fusion.4
  370.7 2.5 fusion.200
  387.2 2.5 multiply_convert_fusion.4
  390.5 2.5 fusion.200
  398.6 5.5 convolution_bitcast_fusion
  404.2 5.2 fusion.98
  409.4 5.8 copy.169
  415.2 10.7 %reshape.285 = f32[2359296]{0:T(1024)} reshape(f32[3072,768]{1,0:T(8,128)} %convolution_bitcast_fusion.1) | data formatting | bytes 18874368 | tf_op jit(solution)/shard_map/reshape | solution.py:246
  425.9 7.9 reshape.282
  433.8 3.4 reshape.283
  438.1 3.8 multiply_reduce_fusion.6
  442.0 4.7 fusion.97
  446.6 3.1 fusion.83
  449.8 14.8 %pad_maximum_fusion = f32[4718592]{0:T(1024)} fusion(f32[2359296]{0:T(1024)S(1)} %copy-done.8, f32[2359296]{0:T(1024)} %bitcast.200), kind=kLoop, calls=%fused_computation.52 | loop fusion | flops 4718592 | bytes 37748736 | tf_op jit(solution)/shard_map/concatenate | solution.py:246
  464.6 6.6 pad_maximum_fusion.1
  474.6 3.6 all-to-all-start.4
  480.4 52.3 %all-to-all-done.4 = bf16[3,256,768]{2,0,1:T(4,128)(2,1)S(1)} async-done(((bf16[3,256,768]{2,0,1:T(4,128)(2,1)}), bf16[3,256,768]{2,0,1:T(4,128)(2,1)S(1)}, u32[]{:S(2)}, u32[]{:S(2)}) %all-to-all-start.4) | async-done | bytes 1179680 | tf_op jit(solution)/shard_map/all_to_all | solution.py:288
  532.7 4.4 all-to-all-start.2
  537.3 74.4 %psum.14 = f32[5,768]{1,0:T(8,128)S(1)} all-reduce(f32[5,768]{1,0:T(8,128)S(1)} %stack.23), channel_id=1, replica_groups=mesh['rows'=8,'seq'=4] {'rows','seq'}, use_global_device_ids=true, to_apply=%region_32.33 | all-reduce | flops 3840 | bytes 30720 | tf_op jit(solution)/shard_map/psum | solution.py:285
  612.3 2.8 copy.145
  615.1 2.7 copy.131
  617.8 390.7 %all-reduce.5.cloned.1.call-done = (f32[2359296]{0:T(1024)}, f32[4718592]{0:T(1024)}, f32[1000,768]{1,0:T(8,128)}) async-done(((f32[2359296]{0:T(1024)}, f32[4718592]{0:T(1024)}, f32[1000,768]{1,0:T(8,128)}), (f32[2359296]{0:T(1024)}, f32[4718592]{0:T(1024)}, f32[1000,768]{1,0:T(8,128)})) %all-reduce.5.cloned.1.call-update) | async-done | bytes 31383568
  1008.5 6.8 multiply_subtract_fusion
  1015.4 2.8 fusion.101
  (340 shorter events, 123.6 us)
Async XLA Ops:
  7.2 16.1 %copy-start.20 = (bf16[12,64,768]{2,1,0:T(8,128)(2,1)S(1)}, bf16[12,64,768]{2,1,0:T(8,128)(2,1)}, u32[]{:S(2)}) copy-start(bf16[12,64,768]{2,1,0:T(8,128)(2,1)} %param.22) | copy-start | bytes 3538948
  7.2 98.4 %all-gather.3.cloned.1.call-start = ((), (), s32[]{:S(2)}) async-start(), calls=%async_computation.5 | async-start | bytes 4866048 | tf_op jit(solution)/shard_map/all_gather | solution.py:161
  9.0 172.9 %all-gather.5.cloned.1.call-start = ((), (), s32[]{:S(2)}) async-start(), calls=%async_computation.6 | async-start | bytes 9732096 | tf_op jit(solution)/shard_map/all_gather | solution.py:162
  23.3 42.4 %copy-start.75 = (s32[12]{0:T(128)S(1)}, s32[12]{0:T(128)}, u32[]{:S(2)}) copy-start(s32[12]{0:T(128)} %param.24) | copy-start | bytes 148
  61.9 3.8 copy-start.49
  61.9 42.0 %all-to-all-start.3 = ((bf16[12,64,768]{2,1,0:T(8,128)(2,1)}), bf16[12,64,768]{2,1,0:T(8,128)(2,1)S(1)}, u32[]{:S(2)}, u32[]{:S(2)}) async-start(bf16[12,64,768]{2,1,0:T(8,128)(2,1)} %param.25), calls=%async_computation.3 | async-start | bytes 2359296 | tf_op jit(solution)/shard_map/all_to_all | solution.py:173
  65.6 942.9 %all-reduce.5.cloned.1.call-start = ((), (), s32[]{:S(2)}) async-start(), calls=%async_computation.7 | async-start | bytes 62767104
  69.4 211.8 %copy-start.26 = (f32[3,768]{1,0:T(4,128)}, f32[3,768]{1,0:T(4,128)S(1)}, u32[]{:S(2)}) copy-start(f32[3,768]{1,0:T(4,128)S(1)} %fusion.84) | copy-start | bytes 27652
  70.0 258.0 %copy-start.28 = (f32[3,256]{1,0:T(4,128)}, f32[3,256]{1,0:T(4,128)S(1)}, u32[]{:S(2)}) copy-start(f32[3,256]{1,0:T(4,128)S(1)} %reshape.286) | copy-start | bytes 9220
  70.1 211.1 %copy-start.1 = (bf16[4,3,64,768]{3,2,0,1:T(8,128)(2,1)}, bf16[4,3,64,768]{3,2,0,1:T(8,128)(2,1)S(1)}, u32[]{:S(2)}) copy-start(bf16[4,3,64,768]{3,2,0,1:T(8,128)(2,1)S(1)} %copy.123) | copy-start | bytes 3538948
  125.6 3.8 copy-start.53
  125.7 3.8 copy-start.59
  125.7 3.8 copy-start.67
  125.7 3.8 copy-start.71
  125.7 3.8 copy-start.72
  168.4 21.7 %copy-start.65 = (f32[3,256]{1,0:T(4,128)}, f32[3,256]{1,0:T(4,128)S(1)}, u32[]{:S(2)}) copy-start(f32[3,256]{1,0:T(4,128)S(1)} %broadcast_multiply_fusion.3) | copy-start | bytes 9220
  216.0 15.8 %copy-start.6 = (f32[4,3,64,768]{3,2,0,1:T(8,128)S(1)}, f32[4,3,64,768]{3,2,0,1:T(8,128)}, u32[]{:S(2)}) copy-start(f32[4,3,64,768]{3,2,0,1:T(8,128)} %copy.132) | copy-start | bytes 7077892
  233.4 5.0 copy-start.35
  234.1 4.2 copy-start.38
  284.3 7.2 slice-start.9
  285.0 6.5 slice-start.10
  285.0 6.5 copy-start.25
  285.0 37.3 %slice-start.5 = ((s8[4718592]{0:T(1024)(128)(4,1)}), s8[4194304]{0:T(1024)(128)(4,1)S(1)}, s32[]{:S(2)}) async-start(s8[4718592]{0:T(1024)(128)(4,1)} %bitcast.217), calls=%async_computation.13 | async-start | bytes 8388608
  291.5 30.7 %slice-start.6 = ((s8[4718592]{0:T(1024)(128)(4,1)}), s8[524288]{0:T(1024)(128)(4,1)S(1)}, s32[]{:S(2)}) async-start(s8[4718592]{0:T(1024)(128)(4,1)} %bitcast.217), calls=%async_computation.14 | async-start | bytes 1048576
  315.1 7.1 copy-start.64
  337.2 4.1 copy-start.3
  341.3 6.3 copy-start
  357.0 4.1 copy-start.3
  361.1 6.3 copy-start
  376.8 4.1 copy-start.3
  380.9 6.3 copy-start
  398.6 5.6 copy-start.15
  398.6 5.6 copy-start.54
  398.6 10.8 %slice-start = ((s8[9437184]{0:T(1024)(128)(4,1)}), s8[4194304]{0:T(1024)(128)(4,1)S(1)}, s32[]{:S(2)}) async-start(s8[9437184]{0:T(1024)(128)(4,1)} %bitcast.198), calls=%async_computation.8 | async-start | bytes 8388608
  398.6 10.7 %slice-start.1 = ((s8[9437184]{0:T(1024)(128)(4,1)}), s8[4194304]{0:T(1024)(128)(4,1)S(1)}, s32[]{:S(2)}) async-start(s8[9437184]{0:T(1024)(128)(4,1)} %bitcast.198), calls=%async_computation.9 | async-start | bytes 8388608
  404.1 5.2 slice-start.2
  433.8 8.1 copy-start.10
  437.2 4.7 copy-start.7
  437.2 4.7 copy-start.34
  437.2 4.7 copy-start.37
  437.2 4.7 copy-start.40
  437.2 4.7 copy-start.55
  437.2 4.7 copy-start.57
  441.9 4.7 copy-start.74
  441.9 7.8 copy-start.8
  446.6 17.9 %slice-start.3 = ((s8[7077888]{0:T(1024)(128)(4,1)}), s8[4194304]{0:T(1024)(128)(4,1)S(1)}, s32[]{:S(2)}) async-start(s8[7077888]{0:T(1024)(128)(4,1)} %bitcast.201), calls=%async_computation.11 | async-start | bytes 8388608
  449.8 14.8 %slice-start.4 = ((s8[7077888]{0:T(1024)(128)(4,1)}), s8[2883584]{0:T(1024)(128)(4,1)S(1)}, s32[]{:S(2)}) async-start(s8[7077888]{0:T(1024)(128)(4,1)} %bitcast.201), calls=%async_computation.12 | async-start | bytes 5767168
  449.8 14.8 %copy-start.12 = (f32[589824]{0:T(1024)S(1)}, f32[589824]{0:T(1024)}, u32[]{:S(2)}) copy-start(f32[589824]{0:T(1024)} %reshape.283) | copy-start | bytes 7077892
  472.4 5.8 copy-start.24
  474.6 58.2 %all-to-all-start.4 = ((bf16[3,256,768]{2,0,1:T(4,128)(2,1)}), bf16[3,256,768]{2,0,1:T(4,128)(2,1)S(1)}, u32[]{:S(2)}, u32[]{:S(2)}) async-start(bf16[3,256,768]{2,0,1:T(4,128)(2,1)} %copy.144), calls=%async_computation.4 | async-start | bytes 3145728 | tf_op jit(solution)/shard_map/all_to_all | solution.py:288
  478.2 58.9 %copy-start.63 = (f32[768]{0:T(1024)S(1)}, f32[768]{0:T(1024)}, u32[]{:S(2)}) copy-start(f32[768]{0:T(1024)} %get-tuple-element.208) | copy-start | bytes 9220
  478.2 59.0 %copy-start.66 = (f32[768]{0:T(1024)S(1)}, f32[768]{0:T(1024)}, u32[]{:S(2)}) copy-start(f32[768]{0:T(1024)} %get-tuple-element.205) | copy-start | bytes 9220
  478.2 59.0 %copy-start.70 = (f32[768]{0:T(1024)S(1)}, f32[768]{0:T(1024)}, u32[]{:S(2)}) copy-start(f32[768]{0:T(1024)} %get-tuple-element.210) | copy-start | bytes 9220
  478.2 59.0 %copy-start.69 = (f32[768]{0:T(1024)S(1)}, f32[768]{0:T(1024)}, u32[]{:S(2)}) copy-start(f32[768]{0:T(1024)} %get-tuple-element.203) | copy-start | bytes 9220
  478.2 59.0 %copy-start.68 = (f32[768]{0:T(1024)S(1)}, f32[768]{0:T(1024)}, u32[]{:S(2)}) copy-start(f32[768]{0:T(1024)} %get-tuple-element.209) | copy-start | bytes 9220
  478.2 133.4 %copy-start.50 = (f32[5,768]{1,0:T(8,128)S(1)}, f32[5,768]{1,0:T(8,128)}, u32[]{:S(2)}) copy-start(f32[5,768]{1,0:T(8,128)} %param.32) | copy-start | bytes 46084
  478.2 133.4 %copy-start.61 = (f32[5,768]{1,0:T(8,128)S(1)}, f32[5,768]{1,0:T(8,128)}, u32[]{:S(2)}) copy-start(f32[5,768]{1,0:T(8,128)} %param.33) | copy-start | bytes 46084
  478.3 133.4 %copy-start.62 = (f32[5,768]{1,0:T(8,128)S(1)}, f32[5,768]{1,0:T(8,128)}, u32[]{:S(2)}) copy-start(f32[5,768]{1,0:T(8,128)} %param.34) | copy-start | bytes 46084
  532.7 79.6 %copy-start.13 = (bf16[3,256,768]{2,0,1:T(4,128)(2,1)}, bf16[3,256,768]{2,0,1:T(4,128)(2,1)S(1)}, u32[]{:S(2)}) copy-start(bf16[3,256,768]{2,0,1:T(4,128)(2,1)S(1)} %all-to-all-done.4) | copy-start | bytes 3538948
  532.7 82.4 %all-to-all-start.2 = ((bf16[3,256,768]{2,0,1:T(4,128)(2,1)}), bf16[3,256,768]{2,0,1:T(4,128)(2,1)}, u32[]{:S(2)}, u32[]{:S(2)}) async-start(bf16[3,256,768]{2,0,1:T(4,128)(2,1)} %copy.130), calls=%async_computation.2 | async-start | bytes 3145728 | tf_op jit(solution)/shard_map/all_to_all | solution.py:287
  612.3 396.2 %copy-start.11 = (f32[1000,768]{1,0:T(8,128)S(1)}, f32[1000,768]{1,0:T(8,128)}, u32[]{:S(2)}) copy-start(f32[1000,768]{1,0:T(8,128)} %param.35) | copy-start | bytes 9216004
  1008.5 6.9 copy-start.17
  1008.5 6.9 copy-start.30
  1008.5 6.9 copy-start.31
  (37 other events, 68.1 us)
Sparse Core Ops, SparseCore 0:
  11.4 80.1 all-gather.2
  95.0 86.8 all-gather.4
  471.3 537.1 all-reduce.4
where the time goes:
time: 1030 us
  waiting for transfers between devices  483 us (47%)
  local copies, waits for them, and re-layouts  174 us (17%)
  matrix products  153 us (15%)
  blocking collectives  125 us (12%)
  other arithmetic  64.4 us (6%)
  between operations  15.2 us (1%)
  starting transfers between devices  11.7 us (1%)
    unnamed x4, waiting for transfers between devices  391 us
    psum x1, blocking collectives, local(): norm_grad, time_grad = lax.psum((norm_local, time_local), ('rows', 'seq'))  74.4 us
    all_to_all x1, waiting for transfers between devices, local(): lax.all_to_all(grad_in, 'seq', split_axis=1, concat_axis=0, tiled=True)  52.3 us
    all_to_all x1, blocking collectives, local(): lax.all_to_all(resid_in, 'seq', split_axis=0, concat_axis=1, tiled=True)  38.6 us
    dynamic_slice x36, local copies, waits for them, and re-layouts, attend_whole(): return lax.map(attend_block, (query_rows, key_rows, value_rows))  38.5 us
    all_to_all x1, waiting for transfers between devices, local(): lax.all_to_all(cotangent, 'seq', split_axis=0, concat_axis=1, tiled=True)  28.5 us
    slice x3, local copies, waits for them, and re-layouts, local(): up_matrix = mlp_full[:model_width * FF].reshape(model_width, FF)  24.7 us
    sub x6, matrix products, attend_block(): soft_weights = jax.nn.softmax(scores, axis=-1)  24.1 us
  transfers between devices with their start and end apart: 6, of which 4 were waited for; matrix products, arithmetic and copies ran while one was open for 8% of the time, Pallas kernels for 0%

commit v1 on v0

v1 whole, which is shorter than its diff:
```python
import functools

import jax
import jax.numpy as jnp
from jax import lax
from jax.experimental import pallas as pl
from jax.experimental.pallas import tpu as pltpu
from jax.sharding import PartitionSpec as P

HEAD_DIM = 64
FF = 3072
STEP = 10
NORM_EPSILON = 1e-05
GROUPS = 32
LANES = 128
TILE = 256
ROW_BLOCK = 64
GELU_C = 0.7978845608028654
GELU_A = 0.044715
LOG2E = 1.4426950408889634
BF = jnp.bfloat16
F32 = jnp.float32

NN = (((1,), (0,)), ((), ()))
NT = (((1,), (1,)), ((), ()))
TN = (((0,), (0,)), ((), ()))


def dot(a, b, dims=NN):
    return lax.dot_general(a, b, dims, preferred_element_type=F32)


def norm_stats(h):
    mean = jnp.mean(h, axis=-1, keepdims=True)
    centred = h - mean
    var = jnp.mean(centred * centred, axis=-1, keepdims=True)
    rs = lax.rsqrt(var + NORM_EPSILON)
    return centred * rs, rs


def fold(x):
    return jnp.sum(x.reshape(x.shape[0] // 8, 8, x.shape[1]), axis=0)


def add_small(small, which, x):
    small[which] = small[which] + fold(x)


class Layer:
    def __init__(self, **refs):
        self.__dict__.update(refs)
        self.T, self.D = self.h.shape
        self.L = self.mask.shape[0]
        self.S = self.T // self.L
        self.PAIRS = self.D // LANES
        self.NJ = FF // self.D

    def qkv_part(self, ref, j, c, n):
        rows = ref.shape[1] // 3
        used = self.D // rows
        return ref.at[pl.ds(0, used), pl.ds(pl.multiple_of(j * rows, rows), rows), pl.ds(pl.multiple_of(c, n), n)]

    def out_part(self, ref, c, n):
        rows = ref.shape[1]
        used = self.D // rows
        return ref.at[pl.ds(ref.shape[0] - used, used), :, pl.ds(pl.multiple_of(c, n), n)]

    def up_part(self, ref, j, c, n):
        rows = ref.shape[1] // self.NJ
        used = self.D // rows
        return ref.at[pl.ds(0, used), pl.ds(pl.multiple_of(j * rows, rows), rows), pl.ds(pl.multiple_of(c, n), n)]

    def down_part(self, ref, j, c, n):
        rows = ref.shape[1]
        used = self.D // rows
        return ref.at[pl.ds(ref.shape[0] // 2 + j * used, used), :, pl.ds(pl.multiple_of(c, n), n)]

    def mask_col(self, s, base, n):
        return self.mask[pl.ds(base, n), s : s + 1].astype(F32)

    def embed(self, s):
        def body(i, _):
            base = pl.multiple_of(i * ROW_BLOCK, ROW_BLOCK)
            rows = pl.ds(pl.multiple_of(s * self.L + base, ROW_BLOCK), ROW_BLOCK)
            m = self.mask_col(s, base, ROW_BLOCK)
            h = self.x[rows, :].astype(F32) + m * self.norm[4:5, :] + self.time[s : s + 1, :]
            self.h[rows, :] = h
            xhat, _ = norm_stats(h)
            self.n1[rows, :] = (xhat * self.norm[0:1, :] + self.norm[1:2, :]).astype(BF)
            return 0

        lax.fori_loop(0, self.L // ROW_BLOCK, body, 0)

    def project(self, s):
        per = self.D // TILE
        rows = pl.ds(s * self.L, self.L)

        def body(i, _):
            j, c = lax.div(i, per), lax.rem(i, per) * TILE
            w = self.qkv_part(self.wa, j, c, TILE)[...].reshape(self.D, TILE)
            y = dot(self.n1[rows, :], w)
            self.qkv[rows, pl.ds(pl.multiple_of(i * TILE, TILE), TILE)] = y.astype(BF)
            return 0

        lax.fori_loop(0, 3 * per, body, 0)

    def pair_slices(self, s, p):
        rows = pl.ds(pl.multiple_of(s * self.L, self.L), self.L)
        cols = [pl.ds(pl.multiple_of(k * self.D + p * LANES, LANES), LANES) for k in range(3)]
        return rows, cols

    def half(self, x, hh):
        first = lax.broadcasted_iota(jnp.int32, x.shape, 1) < HEAD_DIM
        zero = jnp.zeros_like(x)
        return jnp.where(first, zero, x) if hh else jnp.where(first, x, zero)

    def attend(self, s, p):
        rows, cols = self.pair_slices(s, p)
        q, k, v = (self.qkv[rows, c] for c in cols)
        total = None
        for hh in range(2):
            sc = dot(self.half(q, hh), k, NT)
            top = jnp.max(sc, axis=-1, keepdims=True)
            e = jnp.exp2((sc - top) * (HEAD_DIM**-0.5 * LOG2E))
            w = (e * (1.0 / jnp.sum(e, axis=-1, keepdims=True))).astype(BF)
            self.soft[s * 2 * self.PAIRS + p * 2 + hh] = w
            o = dot(w, self.half(v, hh))
            total = o if total is None else total + o
        self.att[rows, cols[0]] = total.astype(BF)

    def attend_sequence(self, s):
        def body(p, _):
            self.attend(s, p)
            return 0

        lax.fori_loop(0, self.PAIRS, body, 0)

    def outer(self, s):
        rows = pl.ds(s * self.L, self.L)

        def body(i, _):
            c = i * TILE
            cols = pl.ds(pl.multiple_of(c, TILE), TILE)
            w = self.out_part(self.wa, c, TILE)[...].reshape(self.D, TILE)
            self.mid[rows, cols] = self.h[rows, cols] + dot(self.att[rows, :], w)
            return 0

        lax.fori_loop(0, self.D // TILE, body, 0)

    def second_norm(self, s):
        def body(i, _):
            rows = pl.ds(pl.multiple_of(s * self.L + i * ROW_BLOCK, ROW_BLOCK), ROW_BLOCK)
            xhat, _ = norm_stats(self.mid[rows, :])
            self.n2[rows, :] = (xhat * self.norm[2:3, :] + self.norm[3:4, :]).astype(BF)
            return 0

        lax.fori_loop(0, self.L // ROW_BLOCK, body, 0)

    def up(self):
        per = self.D // TILE

        def body(i, _):
            j, c = lax.div(i, per), lax.rem(i, per) * TILE
            cols = pl.ds(pl.multiple_of(i * TILE, TILE), TILE)
            w = self.up_part(self.wm, j, c, TILE)[...].reshape(self.D, TILE)
            for s in range(self.S):
                rows = pl.ds(s * self.L, self.L)
                u = dot(self.n2[rows, :], w)
                uu = u * u
                t = jnp.tanh(GELU_C * (u * (1.0 + GELU_A * uu)))
                left = 0.5 * (1.0 + t)
                self.act[rows, cols] = (u * left).astype(BF)
                slope = left + (0.5 * GELU_C) * u * (1.0 - t * t) * (1.0 + 3.0 * GELU_A * uu)
                self.du[rows, cols] = slope.astype(BF)
            return 0

        lax.fori_loop(0, self.NJ * per, body, 0)

    def down(self):
        per = self.D // TILE

        def body(i, _):
            c = i * TILE
            cols = pl.ds(pl.multiple_of(c, TILE), TILE)
            for s in range(self.S):
                rows = pl.ds(s * self.L, self.L)
                total = self.mid[rows, cols]
                for j in range(self.NJ):
                    w = self.down_part(self.wm, j, c, TILE)[...].reshape(self.D, TILE)
                    total = total + dot(self.act[rows, pl.ds(j * self.D, self.D)], w)
                self.out[rows, cols] = total.astype(BF)
            return 0

        lax.fori_loop(0, per, body, 0)

    def mask_cotangent(self):
        for s in range(self.S):
            def body(i, _, s=s):
                base = pl.multiple_of(i * ROW_BLOCK, ROW_BLOCK)
                rows = pl.ds(pl.multiple_of(s * self.L + base, ROW_BLOCK), ROW_BLOCK)
                m = self.mask_col(s, base, ROW_BLOCK)
                self.g[rows, :] = (self.g[rows, :].astype(F32) * m).astype(BF)
                return 0

            lax.fori_loop(0, self.L // ROW_BLOCK, body, 0)

    def grad_pre(self):
        per = self.D // TILE

        def body(i, _):
            cols = pl.ds(pl.multiple_of(i * (self.D // 2), self.D // 2), self.D // 2)
            rows_w = self.wm.shape[1]
            used = self.D // 2 // rows_w
            w = self.wm[pl.ds(self.wm.shape[0] // 2 + i * used, used)].reshape(self.D // 2, self.D)
            for s in range(self.S):
                rows = pl.ds(s * self.L, self.L)
                d = dot(self.g[rows, :], w, NT)
                self.du[rows, cols] = (d * self.du[rows, cols].astype(F32)).astype(BF)
            return 0

        lax.fori_loop(0, 2 * self.NJ, body, 0)

    def grad_down(self):
        per = self.D // TILE
        for j in range(self.NJ):
            self.turn[...] = self.act[:, pl.ds(j * self.D, self.D)].T

            def body(i, _, j=j):
                c = pl.multiple_of(i * TILE, TILE)
                y = dot(self.turn[...], self.g[:, pl.ds(c, TILE)])
                ref = self.down_part(self.gm_down, j, c, TILE)
                ref[...] = y.astype(BF).reshape(ref.shape)
                return 0

            lax.fori_loop(0, per, body, 0)

    def grad_up(self):
        per = self.D // TILE
        self.turn[...] = self.n2[...].T

        def body(i, _):
            j, c = lax.div(i, per), lax.rem(i, per) * TILE
            y = dot(self.turn[...], self.du[:, pl.ds(pl.multiple_of(i * TILE, TILE), TILE)])
            ref = self.up_part(self.gm_up, j, c, TILE)
            ref[...] = y.astype(BF).reshape(ref.shape)
            return 0

        lax.fori_loop(0, self.NJ * per, body, 0)

    def grad_normed_two(self):
        rows_w = self.wm.shape[1] // self.NJ
        n = self.D // 2
        used = n // rows_w

        def body(i, _):
            cols = pl.ds(pl.multiple_of(i * n, n), n)
            for s in range(self.S):
                rows = pl.ds(s * self.L, self.L)
                total = None
                for j in range(self.NJ):
                    w = self.wm[pl.ds(i * used, used), pl.ds(j * rows_w, rows_w), :].reshape(n, self.D)
                    y = dot(self.du[rows, pl.ds(j * self.D, self.D)], w, NT)
                    total = y if total is None else total + y
                self.dn[rows, cols] = total
            return 0

        lax.fori_loop(0, 2, body, 0)

    def norm_two_back(self):
        def body(i, _):
            rows = pl.ds(pl.multiple_of(i * ROW_BLOCK, ROW_BLOCK), ROW_BLOCK)
            xhat, rs = norm_stats(self.mid[rows, :])
            dy = self.dn[rows, :]
            add_small(self.small, 5, dy * xhat)
            add_small(self.small, 6, dy)
            e = dy * self.norm[2:3, :]
            back = (e - jnp.mean(e, -1, keepdims=True) - xhat * jnp.mean(e * xhat, -1, keepdims=True)) * rs
            gm = self.g[rows, :].astype(F32) + back
            self.dn[rows, :] = gm
            self.gb[rows, :] = gm.astype(BF)
            return 0

        lax.fori_loop(0, self.T // ROW_BLOCK, body, 0)

    def grad_outer(self):
        self.turn[...] = self.att[...].T

        def body(i, _):
            c = pl.multiple_of(i * TILE, TILE)
            y = dot(self.turn[...], self.gb[:, pl.ds(c, TILE)])
            ref = self.out_part(self.ga, c, TILE)
            ref[...] = y.astype(BF).reshape(ref.shape)
            return 0

        lax.fori_loop(0, self.D // TILE, body, 0)

    def grad_attended(self):
        n = self.D // 2
        rows_w = self.wa.shape[1]
        used = n // rows_w
        first = self.wa.shape[0] - 2 * used

        def body(i, _):
            w = self.wa[pl.ds(first + i * used, used)].reshape(n, self.D)
            for s in range(self.S):
                rows = pl.ds(s * self.L, self.L)
                self.att[rows, pl.ds(pl.multiple_of(i * n, n), n)] = dot(self.gb[rows, :], w, NT).astype(BF)
            return 0

        lax.fori_loop(0, 2, body, 0)

    def attend_back(self, s, p):
        rows, cols = self.pair_slices(s, p)
        q, k, v = (self.qkv[rows, c] for c in cols)
        da = self.att[rows, cols[0]]
        dq = dk = dv = None
        for hh in range(2):
            w = self.soft[s * 2 * self.PAIRS + p * 2 + hh]
            da_h = self.half(da, hh)
            dp = dot(da_h, v, NT)
            wf = w.astype(F32)
            t = wf * dp
            ds = (t - wf * jnp.sum(t, axis=-1, keepdims=True)).astype(BF)
            parts = (dot(ds, self.half(k, hh)), dot(ds, self.half(q, hh), TN), dot(w, da_h, TN))
            dq, dk, dv = parts if dq is None else (dq + parts[0], dk + parts[1], dv + parts[2])
        scale = HEAD_DIM**-0.5
        self.qkv[rows, cols[0]] = (dq * scale).astype(BF)
        self.qkv[rows, cols[1]] = (dk * scale).astype(BF)
        self.qkv[rows, cols[2]] = dv.astype(BF)

    def attend_back_sequence(self, s):
        def body(p, _):
            self.attend_back(s, p)
            return 0

        lax.fori_loop(0, self.PAIRS, body, 0)

    def grad_normed_one(self, s):
        n = self.D // 3
        rows_w = self.wa.shape[1] // 3
        used = n // rows_w
        rows = pl.ds(s * self.L, self.L)

        def body(i, _):
            total = None
            for j in range(3):
                w = self.wa[pl.ds(i * used, used), pl.ds(j * rows_w, rows_w), :].reshape(n, self.D)
                y = dot(self.qkv[rows, pl.ds(j * self.D, self.D)], w, NT)
                total = y if total is None else total + y
            self.mid[rows, pl.ds(pl.multiple_of(i * n, n), n)] = total
            return 0

        lax.fori_loop(0, 3, body, 0)

    def norm_one_back(self, s):
        def body(i, _):
            base = pl.multiple_of(i * ROW_BLOCK, ROW_BLOCK)
            rows = pl.ds(pl.multiple_of(s * self.L + base, ROW_BLOCK), ROW_BLOCK)
            xhat, rs = norm_stats(self.h[rows, :])
            dy = self.mid[rows, :]
            add_small(self.small, 3, dy * xhat)
            add_small(self.small, 4, dy)
            e = dy * self.norm[0:1, :]
            back = (e - jnp.mean(e, -1, keepdims=True) - xhat * jnp.mean(e * xhat, -1, keepdims=True)) * rs
            gs = self.dn[rows, :] + back
            add_small(self.small, s, gs)
            add_small(self.small, 7, gs * self.mask_col(s, base, ROW_BLOCK))
            self.x[rows, :] = gs.astype(BF)
            return 0

        lax.fori_loop(0, self.L // ROW_BLOCK, body, 0)

    def grad_inner(self):
        per = self.D // TILE
        self.turn[...] = self.n1[...].T

        def body(i, _):
            j, c = lax.div(i, per), lax.rem(i, per) * TILE
            y = dot(self.turn[...], self.qkv[:, pl.ds(pl.multiple_of(i * TILE, TILE), TILE)])
            ref = self.qkv_part(self.ga, j, c, TILE)
            ref[...] = y.astype(BF).reshape(ref.shape)
            return 0

        lax.fori_loop(0, 3 * per, body, 0)


def run_all(k):
    for i in range(8):
        k.small[i] = jnp.zeros(k.small.shape[1:], F32)
    for s in range(k.S):
        k.embed(s)
        k.project(s)
        k.attend_sequence(s)
        k.outer(s)
        k.second_norm(s)
    k.up()
    k.down()
    k.mask_cotangent()
    k.grad_pre()
    k.grad_down()
    k.grad_up()
    k.grad_normed_two()
    k.norm_two_back()
    k.grad_outer()
    k.grad_attended()
    for s in range(k.S):
        k.attend_back_sequence(s)
        k.grad_normed_one(s)
        k.norm_one_back(s)
    k.grad_inner()


def compute_kernel(x, mask, g_in, time, norm, wa, wm, out, gin, ga, gm, small, *scratch):
    names = ("g", "h", "n1", "qkv", "att", "mid", "n2", "act", "du", "soft", "dn", "gb", "turn", "sums")
    refs = dict(zip(names, scratch))
    sums = refs.pop("sums")
    pltpu.sync_copy(x, gin)
    pltpu.sync_copy(g_in, refs["g"])
    layer = Layer(
        x=gin, mask=mask, time=time, norm=norm, wa=wa, wm=wm, out=out, ga=ga, gm_down=gm, gm_up=gm, small=sums, **refs
    )
    run_all(layer)
    for i in range(8):
        small[i : i + 1, :] = jnp.sum(sums[i], axis=0, keepdims=True)


def layer_scratch(T, D, S, L):
    heads = D // HEAD_DIM
    return dict(
        h=pltpu.VMEM((T, D), F32),
        n1=pltpu.VMEM((T, D), BF),
        qkv=pltpu.VMEM((T, 3 * D), BF),
        att=pltpu.VMEM((T, D), BF),
        mid=pltpu.VMEM((T, D), F32),
        n2=pltpu.VMEM((T, D), BF),
        act=pltpu.VMEM((T, FF), BF),
        du=pltpu.VMEM((T, FF), BF),
        soft=pltpu.VMEM((S * heads, L, L), BF),
        dn=pltpu.VMEM((T, D), F32),
        gb=pltpu.VMEM((T, D), BF),
        turn=pltpu.VMEM((D, D), BF),
        sums=pltpu.VMEM((8, 8, D), F32),
    )


def pad_rows(x):
    return jnp.pad(x, ((0, 8 - x.shape[0]), (0, 0)))


def rows_split(flat, groups, parts, D):
    return flat.reshape(groups, -1, parts, D).transpose(0, 2, 1, 3).reshape(groups, -1, D)


def rows_join(block, parts, D):
    groups = block.shape[0]
    return block.reshape(groups, parts, -1, D).transpose(0, 2, 1, 3).reshape(-1)


def adamw(master, moment_one, moment_two, gradient, step_rate):
    first_new = 0.5 * moment_one + 0.5 * gradient
    second_new = 0.5 * moment_two + 0.5 * gradient * gradient
    correct = 1.0 - 0.5**STEP
    update = first_new / correct / (jnp.sqrt(second_new / correct) + 1e-08)
    return (master - step_rate * (update + 0.1 * master), first_new, second_new)


def general(
    resid_in,
    mask,
    steps_row,
    cotangent,
    attn_master,
    attn_first,
    attn_second,
    mlp_master,
    mlp_first,
    mlp_second,
    norm_master,
    norm_first,
    norm_second,
    time_master,
    time_first,
    time_second,
):
    D = resid_in.shape[2]
    axes = ("rows", "seq")
    seq_count = lax.axis_size("seq")
    S = resid_in.shape[0] // seq_count
    L = resid_in.shape[1] * seq_count
    T = S * L
    attn_full = lax.all_gather(attn_master.astype(BF), axes, axis=0, tiled=True)
    mlp_full = lax.all_gather(mlp_master.astype(BF), axes, axis=0, tiled=True)
    inner = 3 * D * D
    wide = D * FF
    wa = jnp.concatenate(
        (rows_split(attn_full[:inner], 24, 3, D), attn_full[inner:].reshape(8, -1, D))
    )
    wm = jnp.concatenate((rows_split(mlp_full[:wide], 16, FF // D, D), mlp_full[wide:].reshape(16, -1, D)))
    exchange = functools.partial(lax.all_to_all, axis_name="seq", split_axis=0, concat_axis=1, tiled=True)
    x = exchange(resid_in).reshape(T, D)
    g = exchange(cotangent).reshape(T, D)
    mask_t = jnp.pad(exchange(mask.astype(BF)).T, ((0, 0), (0, LANES - S)))
    steps_use = lax.dynamic_slice_in_dim(steps_row, lax.axis_index("seq") * S, S, 0)
    time_rows = pad_rows(jnp.take(time_master, steps_use, axis=0))
    V = pl.BlockSpec(memory_space=pltpu.VMEM)
    A = pl.BlockSpec(memory_space=pl.ANY)
    shape = jax.ShapeDtypeStruct
    scratch = layer_scratch(T, D, S, L)
    out, gin, ga, gm, small = pl.pallas_call(
        compute_kernel,
        out_shape=(shape((T, D), BF), shape((T, D), BF), shape(wa.shape, BF), shape(wm.shape, BF), shape((8, D), F32)),
        in_specs=[A, V, A, V, V, V, V],
        out_specs=(V,) * 5,
        scratch_shapes=[pltpu.VMEM((T, D), BF)] + list(scratch.values()),
        compiler_params=pltpu.CompilerParams(vmem_limit_bytes=62 << 20),
    )(x, mask_t, g, time_rows, pad_rows(norm_master), wa, wm)
    attn_flat = jnp.concatenate((rows_join(ga[:24], 3, D), ga[24:].reshape(-1))).astype(F32)
    mlp_flat = jnp.concatenate((rows_join(gm[:16], FF // D, D), gm[16:].reshape(-1))).astype(F32)
    attn_grad = lax.psum_scatter(attn_flat, axes, scatter_dimension=0, tiled=True)
    mlp_grad = lax.psum_scatter(mlp_flat, axes, scatter_dimension=0, tiled=True)
    every = lax.all_gather(small, axes, axis=0)
    spread = functools.partial(lax.all_to_all, axis_name="seq", split_axis=1, concat_axis=0, tiled=True)
    return finish(
        spread(out.reshape(S, L, D)),
        spread(gin.reshape(S, L, D)),
        lax.all_gather(steps_row, "rows", axis=0, tiled=True),
        every,
        adamw(attn_master, attn_first, attn_second, attn_grad, 0.05),
        adamw(mlp_master, mlp_first, mlp_second, mlp_grad, 0.03),
        (norm_master, norm_first, norm_second),
        (time_master, time_first, time_second),
        S,
    )


def finish(resid_out, grad_in, steps, every, attn, mlp, norm, time, S):
    D = every.shape[2]
    norm_grad = jnp.sum(every[:, 3:8], axis=0)
    chosen = (jnp.arange(time[0].shape[0], dtype=jnp.int32)[:, None] == steps[None, :]).astype(F32)
    time_grad = jnp.dot(chosen, every[:, :S].reshape(-1, D), precision=lax.Precision.HIGHEST)
    return (
        resid_out,
        grad_in,
        *attn,
        attn[0].astype(BF),
        *mlp,
        mlp[0].astype(BF),
        *adamw(*norm, norm_grad, 0.2),
        *adamw(*time, time_grad, 0.3),
    )


def solution(mesh):
    flat, whole, tokens = P(("rows", "seq")), P(), P("rows", "seq", None)
    return jax.shard_map(
        general,
        mesh=mesh,
        in_specs=(tokens, P("rows", "seq"), P("rows"), tokens) + (flat,) * 6 + (whole,) * 6,
        out_specs=(tokens, tokens) + (flat,) * 8 + (whole,) * 6,
        check_vma=False,
    )
```

time: 1030 us -> 943 us (0.916)
  matrix products: 153 us -> 10.9 us
  Pallas kernels: 0 us -> 112 us
  local copies, waits for them, and re-layouts: 174 us -> 117 us
  blocking collectives: 125 us -> 180 us
  waiting for transfers between devices: 483 us -> 432 us
    all_gather x0 -> x1, blocking collectives: none -> 122 us  [general(): every = lax.all_gather(small, axes, axis=0)]
    dot_general x34 -> x1, matrix products: 123 us -> 10.9 us  [finish(): jnp.dot(chosen, every[:, :S].reshape(-1, D), precision=lax.Precision.HIGH...]
    pallas_call x0 -> x1, Pallas kernels: none -> 112 us  [general(): pl.pallas_call(compute_kernel, out_shape=(shape((T, D), BF), shape((T, D)...]
    unnamed x4, waiting for transfers between devices: 391 us -> 298 us
    psum x1 -> x0, blocking collectives: 74.4 us -> none  [local(): norm_grad, time_grad = lax.psum((norm_local, time_local), ('rows', 'seq'))]
    all_gather x2, waiting for transfers between devices: 11.1 us -> 49.8 us  [the longest x1 49.8 us: general(): mlp_full = lax.all_gather(mlp_master.astype(BF), axes, axis=0, tiled=True)]
    dynamic_slice x37 -> x0, local copies, waits for them, and re-layouts: 38.6 us -> none  [the longest x36 38.5 us: attend_whole(): return lax.map(attend_block, (query_rows, key_rows, value_rows))]
    sub x9 -> x0, matrix products: 30.7 us -> none  [the longest x6 24.1 us: attend_block(): soft_weights = jax.nn.softmax(scores, axis=-1)]
  transfers between devices with their start and end apart: 6 -> 6, of which waited for: 4 -> 4; matrix products, arithmetic and copies ran while one was open for 8% -> 5% of each run, Pallas kernels for 0% -> 0%
where the time goes in v1:
time: 943 us; the launch traced here: 932 us
  waiting for transfers between devices  432 us (46%)
  blocking collectives  180 us (19%)
  local copies, waits for them, and re-layouts  117 us (12%)
  Pallas kernels  112 us (12%)
  other arithmetic  54.5 us (6%)
  between operations  14.8 us (2%)
  matrix products  10.9 us (1%)
  starting transfers between devices  10.8 us (1%)
    unnamed x4, waiting for transfers between devices  298 us
    all_gather x1, blocking collectives, general(): every = lax.all_gather(small, axes, axis=0)  122 us
    pallas_call x1, Pallas kernels, general(): pl.pallas_call(compute_kernel, out_shape=(shape((T, D), BF), shape((T, D)...  112 us
    all_to_all x1, waiting for transfers between devices, general(): spread(out.reshape(S, L, D))  52.8 us
    all_gather x1, waiting for transfers between devices, general(): mlp_full = lax.all_gather(mlp_master.astype(BF), axes, axis=0, tiled=True)  49.8 us
    all_to_all x1, blocking collectives, general(): x = exchange(resid_in).reshape(T, D)  39.3 us
    all_to_all x1, waiting for transfers between devices, general(): g = exchange(cotangent).reshape(T, D)  31.8 us
    reshape x4, local copies, waits for them, and re-layouts, rows_join(): return block.reshape(groups, parts, -1, D).transpose(0, 2, 1, 3).reshape(-1)  26.8 us
  transfers between devices with their start and end apart: 6, of which 4 were waited for; matrix products, arithmetic and copies ran while one was open for 5% of the time, Pallas kernels for 0%

profile of v1, /device:TPU:0, one launch (start us, length us, event | category | flops | bytes accessed | tf_op | source)
XLA Modules:
  0.0 931.6 jit_solution(4717039774435104703)
XLA Ops:
  7.2 0.0 all-gather.4.cloned.1.call-start
  7.2 1.6 convert_element_type.29
  8.9 0.0 all-gather.6.cloned.1.call-start
  9.0 1.8 convert_element_type.30
  10.8 0.7 convert_element_type.28
  11.5 11.7 %all_to_all.85 = bf16[4,3,64]{2,1,0:T(4,128)(2,1)S(1)} all-to-all(bf16[4,3,64]{2,1,0:T(4,128)(2,1)S(1)} %all_to_all.65), channel_id=1, replica_groups=mesh['rows'=8,'seq'=4] {'seq'}, dimensions={0} | all-to-all | bytes 3072 | tf_op jit(solution)/shard_map/all_to_all | solution.py:502
  23.2 39.3 %all_to_all.86 = bf16[12,64,768]{2,1,0:T(8,128)(2,1)S(1)} all-to-all(bf16[12,64,768]{2,1,0:T(8,128)(2,1)} %param.16), channel_id=1, replica_groups=mesh['rows'=8,'seq'=4] {'seq'}, dimensions={0} | all-to-all | bytes 2359296 | tf_op jit(solution)/shard_map/all_to_all | solution.py:500
  62.5 3.5 all-to-all-start.2
  66.1 0.0 all-reduce.9.cloned.1.call-start
  66.1 0.1 compare_and_fusion
  66.2 2.5 gather_fusion
  68.7 0.1 broadcast_select_fusion
  68.7 0.6 pad.13.time
  69.4 0.6 pad.14.norm
  70.0 0.1 copy.47
  70.1 0.7 pad.12.mask
  70.8 1.1 copy.46
  71.9 31.8 %all-to-all-done.2 = bf16[12,64,768]{2,1,0:T(8,128)(2,1)S(1)} async-done(((bf16[12,64,768]{2,1,0:T(8,128)(2,1)}), bf16[12,64,768]{2,1,0:T(8,128)(2,1)S(1)}, u32[]{:S(2)}, u32[]{:S(2)}) %all-to-all-start.2) | async-done | bytes 1179680 | tf_op jit(solution)/shard_map/all_to_all | solution.py:501
  103.7 1.1 copy.48
  104.8 2.0 slice-done
  106.8 5.4 slice.71
  112.2 3.1 copy.49
  115.3 2.4 slice.87
  117.7 3.4 slice.73
  121.0 3.9 pad_maximum_fusion.1.wa
  124.9 49.8 %all-gather.6.cloned.1.call-done = bf16[4718592]{0:T(1024)(128)(2,1)} async-done(((bf16[147456]{0:T(1024)(128)(2,1)}), bf16[4718592]{0:T(1024)(128)(2,1)}) %all-gather.6.cloned.1.call-update) | async-done | bytes 9437200 | tf_op jit(solution)/shard_map/all_gather | solution.py:492
  174.7 8.2 fusion.13
  183.0 9.4 %slice.75 = bf16[16,48,4,768]{3,2,1,0:T(4,128)(2,1)} reshape(bf16[2359296]{0:T(1024)(128)(2,1)} %get-tuple-element.46) | data formatting | bytes 9437184 | tf_op jit(solution)/shard_map/slice | solution.py:498
  192.3 5.3 copy.50
  197.7 9.2 slice.77
  206.9 9.1 pad_maximum_fusion.wm
  216.0 111.7 %shard_map.279 = (bf16[768,768]{1,0:T(8,128)(2,1)}, bf16[768,768]{1,0:T(8,128)(2,1)}, bf16[32,96,768]{2,1,0:T(8,128)(2,1)}, bf16[32,192,768]{2,1,0:T(8,128)(2,1)}, f32[8,768]{1,0:T(8,128)}) custom-call(bf16[768,768]{1,0:T(8,128)(2,1)} %bitcast.49, bf16[256,128]{1,0:T(8,128)(2,1)} %pad.12.mask, bf16[768,768]{1,0:T(8,128)(2,1)} %bitcast.50, ...), custom_call_target="tpu_custom_call" | custom-call | tf_op jit(solution)/shard_map/pallas_call | solution.py:509
  327.7 2.2 slice.78
  329.9 2.4 slice.79
  332.3 6.7 fusion.12
  339.0 4.6 copy.59
  343.6 8.9 reshape.128
  352.5 9.4 %reshape.129 = bf16[2359296]{0:T(1024)(128)(2,1)} reshape(bf16[16,192,768]{2,1,0:T(8,128)(2,1)} %get-tuple-element.45) | data formatting | bytes 9437184 | tf_op jit(solution)/shard_map/reshape | solution.py:518
  361.8 5.4 copy.60
  367.2 7.9 reshape.125
  375.2 3.4 reshape.126
  378.5 13.0 %maximum_convert_fusion = f32[4718592]{0:T(1024)} fusion(bf16[2359296]{0:T(1024)(128)(2,1)} %reshape.129, bf16[2359296]{0:T(1024)(128)(2,1)} %reshape.128), kind=kLoop, calls=%fused_computation.2 | loop fusion | flops 18874368 | bytes 28311552 | tf_op jit(solution)/shard_map/convert_element_type | solution.py:518
  391.6 16.3 %maximum_convert_fusion.1 = f32[2359296]{0:T(1024)} fusion(bf16[589824]{0:T(1024)(128)(2,1)S(1)} %copy-done.1, bf16[1769472]{0:T(1024)(128)(2,1)S(1)} %reshape.125), kind=kLoop, calls=%fused_computation.4 | loop fusion | flops 9437184 | bytes 14155776 | tf_op jit(solution)/shard_map/convert_element_type | solution.py:517
  407.9 1.2 copy-done.4
  409.1 2.2 copy.51
  411.3 3.6 all-to-all-start.3
  414.9 2.1 copy.53
  417.1 52.8 %all-to-all-done.3 = bf16[3,256,768]{2,0,1:T(4,128)(2,1)S(1)} async-done(((bf16[3,256,768]{2,0,1:T(4,128)(2,1)}), bf16[3,256,768]{2,0,1:T(4,128)(2,1)S(1)}, u32[]{:S(2)}, u32[]{:S(2)}) %all-to-all-start.3) | async-done | bytes 1179680 | tf_op jit(solution)/shard_map/all_to_all | solution.py:524
  469.8 3.6 all-to-all-start.4
  473.4 0.6 dynamic-slice
  474.7 0.2 dynamic-update-slice
  474.9 7.3 all-reduce.3
  482.2 121.7 %all-gather = f32[256,768]{1,0:T(8,128)S(1)} all-gather(f32[8,768]{1,0:T(8,128)S(1)} %copy-done.8), channel_id=2, replica_groups=mesh['rows'=8,'seq'=4] {'rows','seq'}, dimensions={0}, use_global_device_ids=true | all-gather | bytes 811008 | tf_op jit(solution)/shard_map/all_gather | solution.py:521
  603.9 0.9 copy-done
  604.8 0.1 slice.91
  604.8 0.9 reshape.130
  605.7 1.3 slice_reduce_fusion
  606.9 1.4 multiply_subtract_fusion.3
  608.3 10.9 %multiply_subtract_fusion = (f32[1000,768]{1,0:T(8,128)}, f32[1000,768]{1,0:T(8,128)}, f32[1000,768]{1,0:T(8,128)}) fusion(f32[1000,768]{1,0:T(8,128)} %param.29, f32[1000,768]{1,0:T(8,128)} %param.30, f32[1000,768]{1,0:T(8,128)} %param.31, f32[96,768]{1,0:T(8,128)} %reshape.130, s32[96]{0:T(128)S(1)} %all-reduce.3), kind=kOutput, calls=%fused_computation.10 | convolution fusion | flops 895584000 | bytes 18727296 | tf_op jit(solution)/shard_map/dot_general | solution.py:540
  619.2 1.2 copy.52
  620.5 1.2 copy.54
  621.7 297.9 %all-reduce.9.cloned.1.call-done = (f32[2359296]{0:T(1024)}, f32[4718592]{0:T(1024)}) async-done(((f32[2359296]{0:T(1024)}, f32[4718592]{0:T(1024)}), (f32[2359296]{0:T(1024)}, f32[4718592]{0:T(1024)})) %all-reduce.9.cloned.1.call-update) | async-done | bytes 28311568
  919.5 3.2 fusion.8
  922.7 2.1 fusion.10
  (29 shorter events, 0.1 us)
Async XLA Ops:
  7.2 58.9 %copy-start.9 = (s32[12]{0:T(128)S(1)}, s32[12]{0:T(128)}, u32[]{:S(2)}) copy-start(s32[12]{0:T(128)} %param.18) | copy-start | bytes 148
  7.2 62.2 %copy-start.7 = (f32[5,768]{1,0:T(8,128)S(1)}, f32[5,768]{1,0:T(8,128)}, u32[]{:S(2)}) copy-start(f32[5,768]{1,0:T(8,128)} %param.26) | copy-start | bytes 46084
  7.2 97.6 %all-gather.4.cloned.1.call-start = ((), (), s32[]{:S(2)}) async-start(), calls=%async_computation.5 | async-start | bytes 4866048 | tf_op jit(solution)/shard_map/all_gather | solution.py:491
  8.9 165.8 %all-gather.6.cloned.1.call-start = ((), (), s32[]{:S(2)}) async-start(), calls=%async_computation.6 | async-start | bytes 9732096 | tf_op jit(solution)/shard_map/all_gather | solution.py:492
  62.5 41.2 %all-to-all-start.2 = ((bf16[12,64,768]{2,1,0:T(8,128)(2,1)}), bf16[12,64,768]{2,1,0:T(8,128)(2,1)S(1)}, u32[]{:S(2)}, u32[]{:S(2)}) async-start(bf16[12,64,768]{2,1,0:T(8,128)(2,1)} %param.19), calls=%async_computation.2 | async-start | bytes 2359296 | tf_op jit(solution)/shard_map/all_to_all | solution.py:501
  66.1 853.5 %all-reduce.9.cloned.1.call-start = ((), (), s32[]{:S(2)}) async-start(), calls=%async_computation.7 | async-start | bytes 56623104
  104.8 2.0 slice-start
  378.5 13.1 %copy-start.1 = (bf16[589824]{0:T(1024)(128)(2,1)S(1)}, bf16[589824]{0:T(1024)(128)(2,1)}, u32[]{:S(2)}) copy-start(bf16[589824]{0:T(1024)(128)(2,1)} %reshape.126) | copy-start | bytes 3538948
  407.9 1.3 copy-start.4
  407.9 7.0 copy-start.3
  411.3 58.5 %all-to-all-start.3 = ((bf16[3,256,768]{2,0,1:T(4,128)(2,1)}), bf16[3,256,768]{2,0,1:T(4,128)(2,1)S(1)}, u32[]{:S(2)}, u32[]{:S(2)}) async-start(bf16[3,256,768]{2,0,1:T(4,128)(2,1)} %copy.51), calls=%async_computation.3 | async-start | bytes 3145728 | tf_op jit(solution)/shard_map/all_to_all | solution.py:524
  414.9 58.5 %copy-start.10 = (u32[32]{0:T(128)S(1)}, u32[32]{0:T(128)}, u32[]{:S(2)}) copy-start(u32[32]{0:T(128)} %constant.78) | copy-start | bytes 388
  414.9 67.3 %copy-start.8 = (f32[8,768]{1,0:T(8,128)S(1)}, f32[8,768]{1,0:T(8,128)}, u32[]{:S(2)}) copy-start(f32[8,768]{1,0:T(8,128)} %get-tuple-element.25) | copy-start | bytes 73732
  469.8 150.6 %all-to-all-start.4 = ((bf16[3,256,768]{2,0,1:T(4,128)(2,1)}), bf16[3,256,768]{2,0,1:T(4,128)(2,1)S(1)}, u32[]{:S(2)}, u32[]{:S(2)}) async-start(bf16[3,256,768]{2,0,1:T(4,128)(2,1)} %copy.53), calls=%async_computation.4 | async-start | bytes 3145728 | tf_op jit(solution)/shard_map/all_to_all | solution.py:525
  603.9 0.9 copy-start
  620.4 302.3 %copy-start.2 = (f32[73728]{0:T(1024)S(1)}, f32[73728]{0:T(1024)}, u32[]{:S(2)}) copy-start(f32[73728]{0:T(1024)} %param.20) | copy-start | bytes 884740
  620.5 302.3 %copy-start.5 = (f32[73728]{0:T(1024)S(1)}, f32[73728]{0:T(1024)}, u32[]{:S(2)}) copy-start(f32[73728]{0:T(1024)} %param.21) | copy-start | bytes 884740
  620.5 302.3 %copy-start.6 = (f32[73728]{0:T(1024)S(1)}, f32[73728]{0:T(1024)}, u32[]{:S(2)}) copy-start(f32[73728]{0:T(1024)} %param.22) | copy-start | bytes 884740
Sparse Core Ops, SparseCore 0:
  11.4 79.4 all-gather.3
  94.3 80.3 all-gather.5
  408.0 511.4 all-reduce.8

commit v2 on v1

--- a/solution.py
+++ b/solution.py
@@ -169,7 +169,7 @@
                 uu = u * u
                 t = jnp.tanh(GELU_C * (u * (1.0 + GELU_A * uu)))
                 left = 0.5 * (1.0 + t)
-                self.act[rows, cols] = (u * left).astype(BF)
+                self.act[pl.ds(pl.multiple_of(j * self.T + s * self.L, self.L), self.L), pl.ds(pl.multiple_of(c, TILE), TILE)] = (u * left).astype(BF)
                 slope = left + (0.5 * GELU_C) * u * (1.0 - t * t) * (1.0 + 3.0 * GELU_A * uu)
                 self.du[rows, cols] = slope.astype(BF)
             return 0
@@ -187,7 +187,7 @@
                 total = self.mid[rows, cols]
                 for j in range(self.NJ):
                     w = self.down_part(self.wm, j, c, TILE)[...].reshape(self.D, TILE)
-                    total = total + dot(self.act[rows, pl.ds(j * self.D, self.D)], w)
+                    total = total + dot(self.act[pl.ds(j * self.T + s * self.L, self.L), :], w)
                 self.out[rows, cols] = total.astype(BF)
             return 0
 
@@ -223,7 +223,7 @@
     def grad_down(self):
         per = self.D // TILE
         for j in range(self.NJ):
-            self.turn[...] = self.act[:, pl.ds(j * self.D, self.D)].T
+            self.turn[...] = self.act[pl.ds(j * self.T, self.T), :].T
 
             def body(i, _, j=j):
                 c = pl.multiple_of(i * TILE, TILE)
@@ -410,6 +410,261 @@
     k.grad_inner()
 
 
+def flip(index, bit):
+    return index + bit - 2 * bit * lax.rem(lax.div(index, bit), 2)
+
+
+def pick(table, index):
+    value = table[0]
+    for i in range(1, len(table)):
+        value = jnp.where(index == i, table[i], value)
+    return value
+
+
+class Links:
+    def __init__(self, Z, S, part):
+        self.Z, self.S, self.part = Z, S, part
+        self.r, self.z = lax.axis_index("rows"), lax.axis_index("seq")
+        r = self.r
+        self.core, self.xn, self.yn = flip(r, 1), flip(r, 2), flip(r, 4)
+        self.diag = flip(self.xn, 4)
+        self.pending = []
+        orders = [sorted(range(Z), key=lambda a: (abs(a - z), a)) for z in range(Z)]
+        self.order = [pick([orders[z][i] for z in range(Z)], self.z) for i in range(Z)]
+        self.has_right, self.has_left = self.z < Z - 1, self.z > 0
+
+    def barrier(self):
+        bar = pltpu.get_barrier_semaphore()
+        peers = [(self.core, self.z), (self.xn, self.z), (self.yn, self.z)]
+        peers += [(self.r, lax.rem(self.z + i, self.Z)) for i in range(1, self.Z)]
+        for peer in peers:
+            pl.semaphore_signal(bar, 1, device_id=peer, device_id_type=pl.DeviceIdType.MESH)
+        pl.semaphore_wait(bar, len(peers))
+
+    def send(self, src, dst, ss, rs, peer, cond=None):
+        copy = pltpu.make_async_remote_copy(
+            src, dst, ss, rs, device_id=peer, device_id_type=pl.DeviceIdType.MESH
+        )
+        if cond is None:
+            copy.start()
+        else:
+            pl.when(cond)(copy.start)
+        self.pending.append((cond, copy))
+
+    def arrived(self, dst, rs, cond=None):
+        copy = pltpu.make_async_remote_copy(
+            dst, dst, rs, rs, device_id=(self.core, self.z), device_id_type=pl.DeviceIdType.MESH
+        )
+        if cond is None:
+            copy.wait_recv()
+        else:
+            pl.when(cond)(copy.wait_recv)
+
+    def flush(self, kept=0):
+        for cond, copy in self.pending[kept:]:
+            if cond is None:
+                copy.wait_send()
+            else:
+                pl.when(cond)(copy.wait_send)
+        del self.pending[kept:]
+
+    def gather(self, w, ss, rs):
+        Z, z = self.Z, self.z
+        count = [0]
+
+        def go(row, zz, peer, cond=None):
+            i = row * Z + zz
+            self.send(w.at[i], w.at[i], ss.at[count[0]], rs.at[i], peer, cond)
+            count[0] += 1
+
+        def got(row, zz):
+            i = row * Z + zz
+            self.arrived(w.at[i], rs.at[i])
+
+        def own(i):
+            zz = self.order[i]
+            if i:
+                got(self.r, zz)
+            go(self.r, zz, (self.r, z + 1), jnp.logical_and(zz <= z, self.has_right))
+            go(self.r, zz, (self.r, z - 1), jnp.logical_and(zz >= z, self.has_left))
+            go(self.r, zz, (self.xn, z))
+            go(self.r, zz, (self.yn, z))
+            go(self.r, zz, (self.core, z))
+
+        def side(i):
+            zz = self.order[i]
+            got(self.xn, zz)
+            go(self.xn, zz, (self.yn, z), zz < Z // 2)
+            got(self.yn, zz)
+            go(self.yn, zz, (self.xn, z), zz >= Z // 2)
+            go(self.xn, zz, (self.core, z))
+            go(self.yn, zz, (self.core, z))
+
+        def far(i):
+            zz = self.order[i]
+            got(self.diag, zz)
+            go(self.diag, zz, (self.core, z))
+
+        def last():
+            for row in (self.r, self.xn, self.yn, self.diag):
+                for i in range(Z):
+                    got(flip(row, 1), self.order[i])
+
+        steps = [functools.partial(own, 0), functools.partial(own, 1)]
+        for i in range(Z):
+            if i + 2 < Z:
+                steps.append(functools.partial(own, i + 2))
+            steps.append(functools.partial(side, i))
+            if i:
+                steps.append(functools.partial(far, i - 1))
+        steps.append(functools.partial(far, Z - 1))
+        steps.append(last)
+        return steps
+
+    def exchange_in(self, src, dst, ss, rs, local, seqs):
+        L = self.part * self.Z
+        for i in seqs:
+            for step in range(1, self.Z):
+                to = lax.rem(self.z + step, self.Z)
+                rows = pl.ds(i * L + self.z * self.part, self.part)
+                n = i * (self.Z - 1) + step - 1
+                self.send(src.at[to * self.S + i], dst.at[rows], ss.at[n], rs.at[n], (self.r, to))
+            rows = pl.ds(i * L + self.z * self.part, self.part)
+            pltpu.make_async_copy(src.at[self.z * self.S + i], dst.at[rows], local.at[i]).start()
+
+    def exchange_in_done(self, src, dst, rs, local, i):
+        L = self.part * self.Z
+        for step in range(1, self.Z):
+            source = lax.rem(self.z + self.Z - step, self.Z)
+            rows = pl.ds(i * L + source * self.part, self.part)
+            self.arrived(dst.at[rows], rs.at[i * (self.Z - 1) + step - 1])
+        rows = pl.ds(i * L + self.z * self.part, self.part)
+        pltpu.make_async_copy(src.at[self.z * self.S + i], dst.at[rows], local.at[i]).wait()
+
+    def exchange_out(self, src, dst, ss, rs, local, i):
+        L = self.part * self.Z
+        for step in range(1, self.Z):
+            to = lax.rem(self.z + step, self.Z)
+            rows = pl.ds(i * L + to * self.part, self.part)
+            n = i * (self.Z - 1) + step - 1
+            self.send(src.at[rows], dst.at[self.z * self.S + i], ss.at[n], rs.at[n], (self.r, to))
+        rows = pl.ds(i * L + self.z * self.part, self.part)
+        pltpu.make_async_copy(src.at[rows], dst.at[self.z * self.S + i], local.at[i]).start()
+
+    def exchange_out_done(self, src, dst, rs, local, i):
+        L = self.part * self.Z
+        for step in range(1, self.Z):
+            source = lax.rem(self.z + self.Z - step, self.Z)
+            self.arrived(dst.at[source * self.S + i], rs.at[i * (self.Z - 1) + step - 1])
+        rows = pl.ds(i * L + self.z * self.part, self.part)
+        pltpu.make_async_copy(src.at[rows], dst.at[self.z * self.S + i], local.at[i]).wait()
+
+    def scatter(self, g, base, inbox, ss, rs, total):
+        Z, z = self.Z, self.z
+        half = Z // 2
+        chip = lax.div(self.r, 2)
+        k = lax.rem(self.r, 2)
+        cx, cy = flip(chip, 1), flip(chip, 2)
+        cd = flip(cx, 2)
+        rows = total.shape[0]
+
+        def block(c, parity, lo, n):
+            return g.at[pl.ds(base + (2 * c + parity) * Z + lo, n)]
+
+        def inslot(i, n):
+            return inbox.at[pl.ds(i, n), pl.ds(0, rows)]
+
+        def add(dst, src, n):
+            def body(i, _):
+                dst[i] = (dst[i].astype(F32) + src[i].astype(F32)).astype(BF)
+                return 0
+
+            lax.fori_loop(0, n, body, 0)
+
+        XY = 4 * Z
+        ZB = XY + 6 * half
+
+        def core_send(c):
+            self.send(block(c, 1 - k, 0, Z), inslot(c * Z, Z), ss.at[c], rs.at[c], (self.core, z))
+
+        def core_add(c):
+            self.arrived(inslot(c * Z, Z), rs.at[c])
+            add(block(c, k, 0, Z), inslot(c * Z, Z), Z)
+
+        def xy_send(slot, c, lo, peer):
+            i = XY + slot * half
+            self.send(block(c, k, lo, half), inslot(i, half), ss.at[4 + slot], rs.at[4 + slot], (peer, z))
+
+        def xy_add(slot, c, lo):
+            i = XY + slot * half
+            self.arrived(inslot(i, half), rs.at[4 + slot])
+            add(block(c, k, lo, half), inslot(i, half), half)
+
+        def first_send():
+            xy_send(0, cd, 0, self.xn)
+            xy_send(2, cd, half, self.yn)
+            xy_send(1, cx, 0, self.xn)
+            xy_send(3, cy, half, self.yn)
+
+        def second():
+            xy_add(0, cy, 0)
+            xy_send(4, cy, 0, self.yn)
+            xy_add(2, cx, half)
+            xy_send(5, cx, half, self.xn)
+
+        def second_own():
+            xy_add(1, chip, 0)
+            xy_add(3, chip, half)
+
+        def third():
+            xy_add(4, chip, 0)
+            xy_add(5, chip, half)
+
+        def line(zz_static):
+            for target, going, back, step, slot in (
+                (zz_static, self.has_right, self.has_left, 1, ZB + zz_static - 1),
+                (Z - 1 - zz_static, self.has_left, self.has_right, -1, ZB + Z - 1 + zz_static - 1),
+            ):
+                sem = 10 + slot - ZB
+                ahead = (target > z) if step == 1 else (target < z)
+                own = block(chip, k, target, 1)
+                box = inslot(slot, 1)
+
+                @pl.when(jnp.logical_and(ahead, back))
+                def _():
+                    self.arrived(box, rs.at[sem])
+                    own[0] = (own[0].astype(F32) + box[0].astype(F32)).astype(BF)
+
+                self.send(own, box, ss.at[sem], rs.at[sem], (self.r, z + step), jnp.logical_and(ahead, going))
+
+        def final():
+            mine = block(chip, k, z, 1)
+            total[...] = mine[0].astype(F32)
+            left = inslot(ZB + z - 1, 1)
+            right = inslot(ZB + Z - 1 + Z - 2 - z, 1)
+
+            @pl.when(self.has_left)
+            def _():
+                self.arrived(left, rs.at[10 + z - 1])
+                total[...] += left[0].astype(F32)
+
+            @pl.when(self.has_right)
+            def _():
+                self.arrived(right, rs.at[10 + Z - 1 + Z - 2 - z])
+                total[...] += right[0].astype(F32)
+
+        return dict(
+            core_send=core_send,
+            core_add=core_add,
+            first_send=first_send,
+            second=second,
+            second_own=second_own,
+            third=third,
+            line=line,
+            final=final,
+        )
+
+
 def compute_kernel(x, mask, g_in, time, norm, wa, wm, out, gin, ga, gm, small, *scratch):
     names = ("g", "h", "n1", "qkv", "att", "mid", "n2", "act", "du", "soft", "dn", "gb", "turn", "sums")
     refs = dict(zip(names, scratch))
@@ -433,7 +688,7 @@
         att=pltpu.VMEM((T, D), BF),
         mid=pltpu.VMEM((T, D), F32),
         n2=pltpu.VMEM((T, D), BF),
-        act=pltpu.VMEM((T, FF), BF),
+        act=pltpu.VMEM((FF // D * T, D), BF),
         du=pltpu.VMEM((T, FF), BF),
         soft=pltpu.VMEM((S * heads, L, L), BF),
         dn=pltpu.VMEM((T, D), F32),
@@ -550,10 +805,266 @@
     )
 
 
+LAYER_REFS = ("h", "n1", "qkv", "att", "mid", "n2", "act", "du", "soft", "dn", "turn", "sums")
+
+
+def whole_kernel(
+    cfg, resid, cot, mask_in, time, norm, sa, sm, resid_out, grad_in, ta, tm, every_out, *scratch
+):
+    Z, S, part = cfg
+    names = (
+        "wa", "wm", "inbox", "x", "g", "mask", "h", "n1",
+        "qkv", "att", "mid", "n2", "act", "du", "soft", "dn",
+        "turn", "sums", "every", "sem_a", "sem_m", "sem_e", "sem_in", "sem_cot",
+        "sem_out", "sem_gin", "sem_mask", "loc", "sem_ra", "sem_rm", "credit",
+    )
+    v = dict(zip(names, scratch))
+    wm, ga = v["wm"], v["act"].reshape(GROUPS, v["wa"].shape[1], v["wa"].shape[2])
+    half = GROUPS // 2
+    grads = wm.at[pl.ds(half, GROUPS)]
+    k = Layer(
+        x=v["x"], out=v["x"], g=v["g"], mask=v["mask"], time=time, norm=norm, wa=v["wa"], wm=wm.at[pl.ds(0, GROUPS)],
+        ga=ga, gm_up=grads, gm_down=grads, small=v["sums"], gb=v["n2"],
+        **{n: v[n] for n in LAYER_REFS[:-1]},
+    )
+    net = Links(Z, S, part)
+    me = net.r * Z + net.z
+    loc = v["loc"]
+    own_a = pltpu.make_async_copy(sa, v["wa"].at[me], loc.at[4, 0])
+    own_m = pltpu.make_async_copy(sm, wm.at[me], loc.at[4, 1])
+    own_a.start()
+    own_m.start()
+    for i in range(8):
+        k.small[i] = jnp.zeros(k.small.shape[1:], F32)
+    net.barrier()
+    own_a.wait()
+    own_m.wait()
+
+    def pair(name):
+        return v[name].at[0], v[name].at[1]
+
+    ra = net.gather(v["wa"], *pair("sem_a"))
+    rm = net.gather(wm, *pair("sem_m"))
+    ra.pop(0)()
+    for step in range(1, Z):
+        to = lax.rem(net.z + step, Z)
+        rows = pl.ds(net.z * part, part)
+        net.send(mask_in.at[to], k.mask.at[rows], v["sem_mask"].at[0, step], v["sem_mask"].at[1, step], (net.r, to))
+    own_mask = pltpu.make_async_copy(mask_in.at[net.z], k.mask.at[pl.ds(net.z * part, part)], loc.at[4, 2])
+    own_mask.start()
+    net.exchange_in(resid, k.x, *pair("sem_in"), loc.at[0], range(S))
+    rm.pop(0)()
+    while ra:
+        ra.pop(0)()
+        if rm and len(rm) > 3:
+            rm.pop(0)()
+    own_mask.wait()
+    for step in range(1, Z):
+        source = lax.rem(net.z + Z - step, Z)
+        net.arrived(k.mask.at[pl.ds(source * part, part)], v["sem_mask"].at[1, step])
+
+    def pump(events, n=1):
+        for _ in range(n):
+            if events:
+                events.pop(0)()
+
+    net.exchange_in(cot, k.g, *pair("sem_cot"), loc.at[1], range(S))
+    for s in range(S):
+        net.exchange_in_done(resid, k.x, v["sem_in"].at[1], loc.at[0], s)
+        k.embed(s)
+        k.project(s)
+        pump(rm)
+        k.attend_sequence(s)
+        pump(rm)
+        k.outer(s)
+        k.second_norm(s)
+    pump(rm, len(rm))
+    k.up()
+    k.down()
+    net.flush()
+    for s in range(S):
+        net.exchange_out(k.out, resid_out, *pair("sem_out"), loc.at[2], s)
+    for s in range(S):
+        net.exchange_in_done(cot, k.g, v["sem_cot"].at[1], loc.at[1], s)
+    k.mask_cotangent()
+    k.grad_pre()
+    k.grad_down()
+    total_m, total_a = k.mid.at[pl.ds(0, sm.shape[0])], k.mid.at[pl.ds(sm.shape[0], sa.shape[0])]
+    m = net.scatter(wm, half, v["inbox"], *pair("sem_rm"), total_m)
+    m["core_send"](2)
+    m["core_send"](3)
+    k.grad_up()
+    m["core_send"](0)
+    m["core_send"](1)
+    m["core_add"](2)
+    m["core_add"](3)
+    k.grad_normed_two()
+    m["core_add"](0)
+    m["core_add"](1)
+    m["first_send"]()
+    k.norm_two_back()
+    k.grad_outer()
+    k.grad_attended()
+    net.flush()
+    for s in range(S):
+        net.exchange_out_done(k.out, resid_out, v["sem_out"].at[1], loc.at[2], s)
+    k.attend_back_sequence(0)
+    m["second"]()
+    k.grad_normed_one(0)
+    k.norm_one_back(0)
+    net.exchange_out(k.x, grad_in, *pair("sem_gin"), loc.at[3], 0)
+    m["second_own"]()
+    k.attend_back_sequence(1)
+    k.grad_normed_one(1)
+    k.norm_one_back(1)
+    net.exchange_out(k.x, grad_in, *pair("sem_gin"), loc.at[3], 1)
+    m["third"]()
+    m["line"](3)
+    k.attend_back_sequence(2)
+    k.grad_normed_one(2)
+    m["line"](2)
+    k.norm_one_back(2)
+    net.exchange_out(k.x, grad_in, *pair("sem_gin"), loc.at[3], 2)
+    m["line"](1)
+    k.grad_inner()
+    for i in range(8):
+        v["every"][me, i : i + 1, :] = jnp.sum(k.small[i], axis=0, keepdims=True)
+    re = net.gather(v["every"], *pair("sem_e"))
+    m["final"]()
+    credit = v["credit"]
+    mesh_id = pl.DeviceIdType.MESH
+    for peer in (net.core, net.xn, net.yn):
+        pl.semaphore_signal(credit, 1, device_id=(peer, net.z), device_id_type=mesh_id)
+    pl.when(net.has_right)(
+        lambda: pl.semaphore_signal(credit, 1, device_id=(net.r, net.z + 1), device_id_type=mesh_id)
+    )
+    pl.when(net.has_left)(
+        lambda: pl.semaphore_signal(credit, 1, device_id=(net.r, net.z - 1), device_id_type=mesh_id)
+    )
+    pl.semaphore_wait(credit, 3 + jnp.where(net.has_right, 1, 0) + jnp.where(net.has_left, 1, 0))
+    a = net.scatter(ga, 0, v["inbox"], *pair("sem_ra"), total_a)
+    for c in range(4):
+        a["core_send"](c)
+    pump(re, 2)
+    for c in range(4):
+        a["core_add"](c)
+    a["first_send"]()
+    pump(re, 4)
+    a["second"]()
+    a["second_own"]()
+    pump(re, 2)
+    a["third"]()
+    for i in (3, 2, 1):
+        a["line"](i)
+        pump(re, 1)
+    pump(re, len(re))
+    a["final"]()
+    for s in range(S):
+        net.exchange_out_done(k.x, grad_in, v["sem_gin"].at[1], loc.at[3], s)
+    outs = [
+        pltpu.make_async_copy(total_m, tm, loc.at[4, 0]),
+        pltpu.make_async_copy(total_a, ta, loc.at[4, 1]),
+        pltpu.make_async_copy(v["every"], every_out, loc.at[4, 2]),
+    ]
+    for copy in outs:
+        copy.start()
+    for copy in outs:
+        copy.wait()
+    net.flush()
+
+
+def fast(
+    resid_in,
+    mask,
+    steps_row,
+    cotangent,
+    attn_master,
+    attn_first,
+    attn_second,
+    mlp_master,
+    mlp_first,
+    mlp_second,
+    norm_master,
+    norm_first,
+    norm_second,
+    time_master,
+    time_first,
+    time_second,
+):
+    D = resid_in.shape[2]
+    Z = lax.axis_size("seq")
+    R = lax.axis_size("rows")
+    S = resid_in.shape[0] // Z
+    part = resid_in.shape[1]
+    L = part * Z
+    T = S * L
+    device = lax.axis_index("rows") * Z + lax.axis_index("seq")
+    attn_low, mlp_low = attn_master.astype(BF), mlp_master.astype(BF)
+    inner_shards = R * Z * 3 // 4
+    is_inner, is_up = device < inner_shards, device < R * Z // 2
+    sa = jnp.where(is_inner, rows_split(attn_low, 1, 3, D)[0], attn_low.reshape(-1, D))
+    sm = jnp.where(is_up, rows_split(mlp_low, 1, FF // D, D)[0], mlp_low.reshape(-1, D))
+    mask_in = mask.astype(BF).reshape(Z, S, part).transpose(0, 2, 1)
+    mask_in = jnp.pad(mask_in, ((0, 0), (0, 0), (0, LANES - S)))
+    steps_use = lax.dynamic_slice_in_dim(steps_row, lax.axis_index("seq") * S, S, 0)
+    time_rows = pad_rows(jnp.take(time_master, steps_use, axis=0))
+    V = pl.BlockSpec(memory_space=pltpu.VMEM)
+    A = pl.BlockSpec(memory_space=pl.ANY)
+    shape = jax.ShapeDtypeStruct
+    sc = layer_scratch(T, D, S, L)
+    dma = pltpu.SemaphoreType.DMA
+    scratch = [
+        pltpu.VMEM((GROUPS, *sa.shape), BF),
+        pltpu.VMEM((GROUPS * 3 // 2, *sm.shape), BF),
+        pltpu.VMEM((4 * Z + 6 * (Z // 2) + 2 * (Z - 1), *sm.shape), BF),
+        pltpu.VMEM((T, D), BF),
+        pltpu.VMEM((T, D), BF),
+        pltpu.VMEM((L, LANES), BF),
+        *(sc[n] for n in LAYER_REFS),
+        pltpu.VMEM((R * Z, 8, D), F32),
+        *(dma((2, 40)) for _ in range(3)),
+        *(dma((2, S * (Z - 1))) for _ in range(4)),
+        dma((2, Z)),
+        dma((5, S)),
+        *(dma((2, 16)) for _ in range(2)),
+        pltpu.SemaphoreType.REGULAR,
+    ]
+    resid_out, grad_in, ta, tm, every = pl.pallas_call(
+        functools.partial(whole_kernel, (Z, S, part)),
+        out_shape=(
+            shape(resid_in.shape, BF),
+            shape(resid_in.shape, BF),
+            shape(sa.shape, F32),
+            shape(sm.shape, F32),
+            shape((R * Z, 8, D), F32),
+        ),
+        in_specs=[A, A, A, V, V, A, A],
+        out_specs=(A,) * 5,
+        scratch_shapes=scratch,
+        compiler_params=pltpu.CompilerParams(
+            collective_id=0, has_side_effects=True, vmem_limit_bytes=63 << 20
+        ),
+    )(resid_in, cotangent, mask_in, time_rows, pad_rows(norm_master), sa, sm)
+    attn_grad = jnp.where(is_inner, rows_join(ta[None], 3, D), ta.reshape(-1))
+    mlp_grad = jnp.where(is_up, rows_join(tm[None], FF // D, D), tm.reshape(-1))
+    return finish(
+        resid_out,
+        grad_in,
+        lax.all_gather(steps_row, "rows", axis=0, tiled=True),
+        every,
+        adamw(attn_master, attn_first, attn_second, attn_grad, 0.05),
+        adamw(mlp_master, mlp_first, mlp_second, mlp_grad, 0.03),
+        (norm_master, norm_first, norm_second),
+        (time_master, time_first, time_second),
+        S,
+    )
+
+
 def solution(mesh):
     flat, whole, tokens = P(("rows", "seq")), P(), P("rows", "seq", None)
+    fits = mesh.shape["rows"] * mesh.shape["seq"] == GROUPS and mesh.shape["rows"] == 8
     return jax.shard_map(
-        general,
+        fast if fits else general,
         mesh=mesh,
         in_specs=(tokens, P("rows", "seq"), P("rows"), tokens) + (flat,) * 6 + (whole,) * 6,
         out_specs=(tokens, tokens) + (flat,) * 8 + (whole,) * 6,

time: 943 us -> 337 us (0.36); the launches traced: 932 us -> 337 us
  waiting for transfers between devices: 432 us -> 0 us
  Pallas kernels: 112 us -> 289 us
  blocking collectives: 180 us -> 9.46 us
  local copies, waits for them, and re-layouts: 117 us -> 16.2 us
  other arithmetic: 54.5 us -> 10.8 us
  between operations: 14.8 us -> 1.53 us
  starting transfers between devices: 10.8 us -> 0 us
    unnamed x4 -> x0, waiting for transfers between devices: 298 us -> none
    pallas_call x1, Pallas kernels: 112 us -> 289 us  [fast(): pl.pallas_call(functools.partial(whole_kernel, (Z, S, part)), out_shape=(...]
    all_gather x1 -> x0, blocking collectives: 122 us -> none  [general(): every = lax.all_gather(small, axes, axis=0)]
    all_to_all x3 -> x0, waiting for transfers between devices: 84.6 us -> none  [the longest x1 52.8 us: general(): spread(out.reshape(S, L, D))]
    slice x11 -> x0, local copies, waits for them, and re-layouts: 51.3 us -> none  [the longest x2 17.6 us: general(): mlp_full[:wide]]
    all_to_all x2 -> x0, blocking collectives: 51 us -> none  [the longest x1 39.3 us: general(): x = exchange(resid_in).reshape(T, D)]
    all_gather x2 -> x0, waiting for transfers between devices: 49.8 us -> none  [the longest x1 49.8 us: general(): mlp_full = lax.all_gather(mlp_master.astype(BF), axes, axis=0, tiled=True)]
    convert_element_type x5 -> x3, other arithmetic: 33.5 us -> 2.77 us  [the longest x2 2.07 us: fast(): attn_low, mlp_low = (attn_master.astype(BF), mlp_master.astype(BF))]
  transfers between devices with their start and end apart: 6 -> 0, of which waited for: 4 -> 0; matrix products, arithmetic and copies ran while one was open for 5% -> 0% of each run, Pallas kernels for 0% -> 0%
where the time goes in v2:
time: 337 us
  Pallas kernels  289 us (86%)
  local copies, waits for them, and re-layouts  16.2 us (5%)
  other arithmetic  10.8 us (3%)
  matrix products  9.96 us (3%)
  blocking collectives  9.46 us (3%)
    pallas_call x1, Pallas kernels, fast(): pl.pallas_call(functools.partial(whole_kernel, (Z, S, part)), out_shape=(...  289 us
    dot_general x1, matrix products, finish(): jnp.dot(chosen, every[:, :S].reshape(-1, D), precision=lax.Precision.HIGH...  9.96 us
    unnamed x1, blocking collectives  9.46 us

profile of v2, /device:TPU:0, one launch (start us, length us, event | category | flops | bytes accessed | tf_op | source)
XLA Modules:
  0.0 336.8 jit_solution(12203217085600447741)
XLA Ops:
  0.7 1.2 dynamic-slice
  2.6 0.9 dynamic-update-slice
  3.4 9.5 %all-reduce.3 = s32[96]{0:T(128)S(1)} all-reduce(s32[96]{0:T(128)S(1)} %dynamic-update-slice), channel_id=1, replica_groups=mesh['rows'=8,'seq'=4] {'rows'}, use_global_device_ids=true, to_apply=%add.3 | all-reduce | flops 96 | bytes 768
  12.9 0.7 compare_and_fusion
  13.6 0.7 convert_element_type.22
  14.3 2.4 gather_fusion
  16.8 0.1 broadcast_select_fusion.2
  16.9 0.6 pad.13.time
  17.5 1.3 pad.14.norm
  18.8 0.1 copy.32
  19.0 0.7 pad.12.mask_in
  19.6 1.0 convert_element_type.23
  20.6 0.1 reshape.70
  20.7 0.1 reshape.69
  20.8 0.7 bitcast_select_fusion.1.sa
  21.5 1.1 convert_element_type.24
  22.6 0.3 reshape.72
  22.9 0.1 reshape.71
  23.1 0.0 copy-start.10
  23.1 0.0 copy-start.11
  23.1 0.0 copy-start.12
  23.1 0.8 bitcast_select_fusion.sm
  23.9 0.0 copy-start.4
  23.9 0.0 copy-start.8
  23.9 288.8 %shard_map.279 = (bf16[12,64,768]{2,1,0:T(8,128)(2,1)}, bf16[12,64,768]{2,1,0:T(8,128)(2,1)}, f32[96,768]{1,0:T(8,128)}, f32[192,768]{1,0:T(8,128)}, f32[32,8,768]{2,1,0:T(8,128)}) custom-call(bf16[12,64,768]{2,1,0:T(8,128)(2,1)} %resid.1, bf16[12,64,768]{2,1,0:T(8,128)(2,1)} %cot.1, bf16[4,64,128]{2,1,0:T(8,128)(2,1)} %pad.12.mask_in, f32[8,768]{1,0:T(8,128)} %pad.13.time, ...), custom_call_target="tpu_custom_call" | custom-call | tf_op jit(solution)/shard_map/pallas_call | solution.py:1032
  312.7 0.0 copy-start.5
  312.7 1.3 slice_reduce_fusion
  314.0 0.0 copy-start
  314.0 1.2 slice.7
  315.3 0.9 reshape.77
  316.1 0.0 copy-done.10
  316.1 0.0 copy-done.11
  316.1 0.0 copy-done.12
  316.1 0.6 multiply_subtract_fusion.3
  316.8 1.0 reshape.74
  317.8 0.0 copy-done.5
  317.8 0.2 copy.40
  318.0 0.2 reshape.73
  318.1 0.0 copy-done.4
  318.2 0.0 copy-done.8
  318.2 0.0 copy-start.1
  318.2 0.0 copy-start.6
  318.2 2.2 fusion.10
  320.4 0.0 copy-start.7
  320.4 0.0 copy-done
  320.4 0.4 copy.39
  320.8 0.2 reshape.75
  321.1 0.0 copy-done.1
  321.1 0.0 copy-done.6
  321.1 0.4 copy-done.7
  321.4 0.0 copy-start.9
  321.4 0.0 copy-start.13
  321.4 1.7 fusion.8
  323.1 0.0 copy-done.9
  323.1 1.1 copy-done.13
  324.2 0.0 copy-start.3
  324.2 10.0 %multiply_subtract_fusion = (f32[1000,768]{1,0:T(8,128)}, f32[1000,768]{1,0:T(8,128)}, f32[1000,768]{1,0:T(8,128)}) fusion(f32[1000,768]{1,0:T(8,128)S(1)} %copy-done.13, f32[1000,768]{1,0:T(8,128)} %param.30, f32[1000,768]{1,0:T(8,128)} %param.31, f32[96,768]{1,0:T(8,128)S(1)} %copy-done.9, s32[96]{0:T(128)S(1)} %all-reduce.3), kind=kOutput, calls=%fused_computation.4 | convolution fusion | flops 895584000 | bytes 18727296 | tf_op jit(solution)/shard_map/dot_general | solution.py:795
  334.1 0.0 copy-start.2
  334.1 0.0 copy-done.3
  334.1 1.0 copy.44
  335.1 0.7 copy-done.2
  335.8 1.0 copy.45
  (6 shorter events, 0.1 us)
Async XLA Ops:
  23.1 293.1 %copy-start.10 = (f32[5,768]{1,0:T(8,128)S(1)}, f32[5,768]{1,0:T(8,128)}, u32[]{:S(2)}) copy-start(f32[5,768]{1,0:T(8,128)} %param.26) | copy-start | bytes 46084
  23.1 293.1 %copy-start.11 = (f32[5,768]{1,0:T(8,128)S(1)}, f32[5,768]{1,0:T(8,128)}, u32[]{:S(2)}) copy-start(f32[5,768]{1,0:T(8,128)} %param.27) | copy-start | bytes 46084
  23.1 293.0 %copy-start.12 = (f32[5,768]{1,0:T(8,128)S(1)}, f32[5,768]{1,0:T(8,128)}, u32[]{:S(2)}) copy-start(f32[5,768]{1,0:T(8,128)} %param.28) | copy-start | bytes 46084
  23.9 294.3 %copy-start.4 = (f32[73728]{0:T(1024)S(1)}, f32[73728]{0:T(1024)}, u32[]{:S(2)}) copy-start(f32[73728]{0:T(1024)} %param.20) | copy-start | bytes 884740
  23.9 294.3 %copy-start.8 = (f32[73728]{0:T(1024)S(1)}, f32[73728]{0:T(1024)}, u32[]{:S(2)}) copy-start(f32[73728]{0:T(1024)} %param.21) | copy-start | bytes 884740
  312.7 5.1 %copy-start.5 = (f32[96,768]{1,0:T(8,128)S(1)}, f32[96,768]{1,0:T(8,128)}, u32[]{:S(2)}) copy-start(f32[96,768]{1,0:T(8,128)} %get-tuple-element.23) | copy-start | bytes 884740
  314.0 6.4 %copy-start = (f32[192,768]{1,0:T(8,128)S(1)}, f32[192,768]{1,0:T(8,128)}, u32[]{:S(2)}) copy-start(f32[192,768]{1,0:T(8,128)} %get-tuple-element.24) | copy-start | bytes 1769476
  318.2 2.9 copy-start.1
  318.2 2.9 copy-start.6
  320.4 1.1 copy-start.7
  321.4 1.7 copy-start.9
  321.4 2.7 copy-start.13
  324.2 10.0 %copy-start.3 = (bf16[12,64,768]{2,1,0:T(8,128)(2,1)S(1)}, bf16[12,64,768]{2,1,0:T(8,128)(2,1)}, u32[]{:S(2)}) copy-start(bf16[12,64,768]{2,1,0:T(8,128)(2,1)} %get-tuple-element.58) | copy-start | bytes 3538948
  334.1 1.7 copy-start.2

commit v3 on v2

--- a/solution.py
+++ b/solution.py
@@ -220,23 +220,37 @@
 
         lax.fori_loop(0, 2 * self.NJ, body, 0)
 
-    def grad_down(self):
+    def turn_activated(self):
+        for j in range(self.NJ):
+            rows = pl.ds(j * self.T, self.T)
+            self.turn[...] = self.act[rows, :].T
+            self.act[rows, :] = self.turn[...]
+        self.turn[...] = self.n2[...].T
+
+    def grad_down(self, part, parts):
+        group = self.gm_down.shape[1]
+        used = self.D // group
+        n = group // parts
         per = self.D // TILE
-        for j in range(self.NJ):
-            self.turn[...] = self.act[pl.ds(j * self.T, self.T), :].T
-
-            def body(i, _, j=j):
-                c = pl.multiple_of(i * TILE, TILE)
-                y = dot(self.turn[...], self.g[:, pl.ds(c, TILE)])
-                ref = self.down_part(self.gm_down, j, c, TILE)
-                ref[...] = y.astype(BF).reshape(ref.shape)
-                return 0
-
-            lax.fori_loop(0, per, body, 0)
-
-    def grad_up(self):
+
+        def body(i, _):
+            j, c = lax.div(i, per), pl.multiple_of(lax.rem(i, per) * TILE, TILE)
+            a = jnp.concatenate(
+                [
+                    self.act[pl.ds(pl.multiple_of(j * self.D + u * group + part * n, 16), n), :]
+                    for u in range(used)
+                ]
+            )
+            y = dot(a, self.g[:, pl.ds(c, TILE)]).astype(BF)
+            ref = self.gm_down.at[pl.ds(self.gm_down.shape[0] // 2 + j * used, used), pl.ds(part * n, n), pl.ds(c, TILE)]
+            ref[...] = y.reshape(used, n, TILE)
+            return 0
+
+        lax.fori_loop(0, self.NJ * per, body, 0)
+
+    def grad_up(self, part, parts):
         per = self.D // TILE
-        self.turn[...] = self.n2[...].T
+        n = self.NJ * per // parts
 
         def body(i, _):
             j, c = lax.div(i, per), lax.rem(i, per) * TILE
@@ -245,7 +259,7 @@
             ref[...] = y.astype(BF).reshape(ref.shape)
             return 0
 
-        lax.fori_loop(0, self.NJ * per, body, 0)
+        lax.fori_loop(part * n, (part + 1) * n, body, 0)
 
     def grad_normed_two(self):
         rows_w = self.wm.shape[1] // self.NJ
@@ -397,8 +411,9 @@
     k.down()
     k.mask_cotangent()
     k.grad_pre()
-    k.grad_down()
-    k.grad_up()
+    k.turn_activated()
+    k.grad_down(0, 1)
+    k.grad_up(0, 1)
     k.grad_normed_two()
     k.norm_two_back()
     k.grad_outer()
@@ -429,9 +444,9 @@
         self.core, self.xn, self.yn = flip(r, 1), flip(r, 2), flip(r, 4)
         self.diag = flip(self.xn, 4)
         self.pending = []
-        orders = [sorted(range(Z), key=lambda a: (abs(a - z), a)) for z in range(Z)]
-        self.order = [pick([orders[z][i] for z in range(Z)], self.z) for i in range(Z)]
-        self.has_right, self.has_left = self.z < Z - 1, self.z > 0
+        near, far = flip(self.z, 1), flip(self.z, 2)
+        self.near, self.far = near, far
+        self.order = [self.z, near, far, flip(near, 2)]
 
     def barrier(self):
         bar = pltpu.get_barrier_semaphore()
@@ -441,7 +456,7 @@
             pl.semaphore_signal(bar, 1, device_id=peer, device_id_type=pl.DeviceIdType.MESH)
         pl.semaphore_wait(bar, len(peers))
 
-    def send(self, src, dst, ss, rs, peer, cond=None):
+    def send(self, src, dst, ss, rs, peer, cond=None, owner=None):
         copy = pltpu.make_async_remote_copy(
             src, dst, ss, rs, device_id=peer, device_id_type=pl.DeviceIdType.MESH
         )
@@ -449,7 +464,7 @@
             copy.start()
         else:
             pl.when(cond)(copy.start)
-        self.pending.append((cond, copy))
+        self.pending.append((owner, cond, copy))
 
     def arrived(self, dst, rs, cond=None):
         copy = pltpu.make_async_remote_copy(
@@ -460,13 +475,17 @@
         else:
             pl.when(cond)(copy.wait_recv)
 
-    def flush(self, kept=0):
-        for cond, copy in self.pending[kept:]:
-            if cond is None:
+    def flush(self, src=None):
+        left = []
+        for item in self.pending:
+            owner, cond, copy = item
+            if src is not None and owner is not src:
+                left.append(item)
+            elif cond is None:
                 copy.wait_send()
             else:
                 pl.when(cond)(copy.wait_send)
-        del self.pending[kept:]
+        self.pending = left
 
     def gather(self, w, ss, rs):
         Z, z = self.Z, self.z
@@ -474,7 +493,7 @@
 
         def go(row, zz, peer, cond=None):
             i = row * Z + zz
-            self.send(w.at[i], w.at[i], ss.at[count[0]], rs.at[i], peer, cond)
+            self.send(w.at[i], w.at[i], ss.at[count[0]], rs.at[i], peer, cond, w)
             count[0] += 1
 
         def got(row, zz):
@@ -485,8 +504,10 @@
             zz = self.order[i]
             if i:
                 got(self.r, zz)
-            go(self.r, zz, (self.r, z + 1), jnp.logical_and(zz <= z, self.has_right))
-            go(self.r, zz, (self.r, z - 1), jnp.logical_and(zz >= z, self.has_left))
+            if i == 0:
+                go(self.r, zz, (self.r, self.far))
+            if i == 0 or i == 2:
+                go(self.r, zz, (self.r, self.near))
             go(self.r, zz, (self.xn, z))
             go(self.r, zz, (self.yn, z))
             go(self.r, zz, (self.core, z))
@@ -510,16 +531,7 @@
                 for i in range(Z):
                     got(flip(row, 1), self.order[i])
 
-        steps = [functools.partial(own, 0), functools.partial(own, 1)]
-        for i in range(Z):
-            if i + 2 < Z:
-                steps.append(functools.partial(own, i + 2))
-            steps.append(functools.partial(side, i))
-            if i:
-                steps.append(functools.partial(far, i - 1))
-        steps.append(functools.partial(far, Z - 1))
-        steps.append(last)
-        return steps
+        return own, side, far, last
 
     def exchange_in(self, src, dst, ss, rs, local, seqs):
         L = self.part * self.Z
@@ -547,7 +559,7 @@
             to = lax.rem(self.z + step, self.Z)
             rows = pl.ds(i * L + to * self.part, self.part)
             n = i * (self.Z - 1) + step - 1
-            self.send(src.at[rows], dst.at[self.z * self.S + i], ss.at[n], rs.at[n], (self.r, to))
+            self.send(src.at[rows], dst.at[self.z * self.S + i], ss.at[n], rs.at[n], (self.r, to), None, dst)
         rows = pl.ds(i * L + self.z * self.part, self.part)
         pltpu.make_async_copy(src.at[rows], dst.at[self.z * self.S + i], local.at[i]).start()
 
@@ -559,7 +571,7 @@
         rows = pl.ds(i * L + self.z * self.part, self.part)
         pltpu.make_async_copy(src.at[rows], dst.at[self.z * self.S + i], local.at[i]).wait()
 
-    def scatter(self, g, base, inbox, ss, rs, total):
+    def scatter(self, g, base, part, inbox, box0, ss, rs, total):
         Z, z = self.Z, self.z
         half = Z // 2
         chip = lax.div(self.r, 2)
@@ -569,10 +581,10 @@
         rows = total.shape[0]
 
         def block(c, parity, lo, n):
-            return g.at[pl.ds(base + (2 * c + parity) * Z + lo, n)]
+            return g.at[pl.ds(base + (2 * c + parity) * Z + lo, n), pl.ds(part * rows, rows)]
 
         def inslot(i, n):
-            return inbox.at[pl.ds(i, n), pl.ds(0, rows)]
+            return inbox.at[pl.ds(box0 + i, n)]
 
         def add(dst, src, n):
             def body(i, _):
@@ -584,6 +596,10 @@
         XY = 4 * Z
         ZB = XY + 6 * half
 
+        def core_send_all():
+            for c in range(4):
+                core_send(c)
+
         def core_send(c):
             self.send(block(c, 1 - k, 0, Z), inslot(c * Z, Z), ss.at[c], rs.at[c], (self.core, z))
 
@@ -600,11 +616,15 @@
             self.arrived(inslot(i, half), rs.at[4 + slot])
             add(block(c, k, lo, half), inslot(i, half), half)
 
-        def first_send():
+        def first():
+            core_add(cd)
             xy_send(0, cd, 0, self.xn)
             xy_send(2, cd, half, self.yn)
+            core_add(cx)
             xy_send(1, cx, 0, self.xn)
+            core_add(cy)
             xy_send(3, cy, half, self.yn)
+            core_add(chip)
 
         def second():
             xy_add(0, cy, 0)
@@ -620,49 +640,26 @@
             xy_add(4, chip, 0)
             xy_add(5, chip, half)
 
-        def line(zz_static):
-            for target, going, back, step, slot in (
-                (zz_static, self.has_right, self.has_left, 1, ZB + zz_static - 1),
-                (Z - 1 - zz_static, self.has_left, self.has_right, -1, ZB + Z - 1 + zz_static - 1),
-            ):
-                sem = 10 + slot - ZB
-                ahead = (target > z) if step == 1 else (target < z)
-                own = block(chip, k, target, 1)
-                box = inslot(slot, 1)
-
-                @pl.when(jnp.logical_and(ahead, back))
-                def _():
-                    self.arrived(box, rs.at[sem])
-                    own[0] = (own[0].astype(F32) + box[0].astype(F32)).astype(BF)
-
-                self.send(own, box, ss.at[sem], rs.at[sem], (self.r, z + step), jnp.logical_and(ahead, going))
+        def z_send(slot, target, peer):
+            box = inslot(ZB + slot, 1)
+            self.send(block(chip, k, target, 1), box, ss.at[10 + slot], rs.at[10 + slot], (self.r, peer))
+
+        def z_first():
+            z_send(1, self.order[3], self.near)
+            z_send(0, self.near, self.near)
+
+        def z_second():
+            self.arrived(inslot(ZB + 1, 1), rs.at[11])
+            add(block(chip, k, self.far, 1), inslot(ZB + 1, 1), 1)
+            z_send(2, self.far, self.far)
 
         def final():
-            mine = block(chip, k, z, 1)
-            total[...] = mine[0].astype(F32)
-            left = inslot(ZB + z - 1, 1)
-            right = inslot(ZB + Z - 1 + Z - 2 - z, 1)
-
-            @pl.when(self.has_left)
-            def _():
-                self.arrived(left, rs.at[10 + z - 1])
-                total[...] += left[0].astype(F32)
-
-            @pl.when(self.has_right)
-            def _():
-                self.arrived(right, rs.at[10 + Z - 1 + Z - 2 - z])
-                total[...] += right[0].astype(F32)
-
-        return dict(
-            core_send=core_send,
-            core_add=core_add,
-            first_send=first_send,
-            second=second,
-            second_own=second_own,
-            third=third,
-            line=line,
-            final=final,
-        )
+            self.arrived(inslot(ZB, 1), rs.at[10])
+            total[...] = block(chip, k, z, 1)[0].astype(F32) + inbox[box0 + ZB].astype(F32)
+            self.arrived(inslot(ZB + 2, 1), rs.at[12])
+            total[...] += inbox[box0 + ZB + 2].astype(F32)
+
+        return core_send_all, first, second, second_own, third, z_first, z_second, final
 
 
 def compute_kernel(x, mask, g_in, time, norm, wa, wm, out, gin, ga, gm, small, *scratch):
@@ -816,7 +813,7 @@
         "wa", "wm", "inbox", "x", "g", "mask", "h", "n1",
         "qkv", "att", "mid", "n2", "act", "du", "soft", "dn",
         "turn", "sums", "every", "sem_a", "sem_m", "sem_e", "sem_in", "sem_cot",
-        "sem_out", "sem_gin", "sem_mask", "loc", "sem_ra", "sem_rm", "credit",
+        "sem_out", "sem_gin", "sem_mask", "loc", "sem_ra", "sem_rm", "credit", "total",
     )
     v = dict(zip(names, scratch))
     wm, ga = v["wm"], v["act"].reshape(GROUPS, v["wa"].shape[1], v["wa"].shape[2])
@@ -843,32 +840,53 @@
     def pair(name):
         return v[name].at[0], v[name].at[1]
 
-    ra = net.gather(v["wa"], *pair("sem_a"))
-    rm = net.gather(wm, *pair("sem_m"))
-    ra.pop(0)()
+    def pump(events, n=1):
+        for _ in range(n):
+            if events:
+                events.pop(0)()
+
+    a_own, a_side, a_far, a_last = net.gather(v["wa"], *pair("sem_a"))
+    m_own, m_side, m_far, m_last = net.gather(wm, *pair("sem_m"))
+
+    def stream(s):
+        net.exchange_in(resid, k.x, *pair("sem_in"), loc.at[0], [s])
+
+    a_own(0)
+    m_own(0)
     for step in range(1, Z):
         to = lax.rem(net.z + step, Z)
         rows = pl.ds(net.z * part, part)
         net.send(mask_in.at[to], k.mask.at[rows], v["sem_mask"].at[0, step], v["sem_mask"].at[1, step], (net.r, to))
     own_mask = pltpu.make_async_copy(mask_in.at[net.z], k.mask.at[pl.ds(net.z * part, part)], loc.at[4, 2])
     own_mask.start()
-    net.exchange_in(resid, k.x, *pair("sem_in"), loc.at[0], range(S))
-    rm.pop(0)()
-    while ra:
-        ra.pop(0)()
-        if rm and len(rm) > 3:
-            rm.pop(0)()
+    a_own(1)
+    a_side(0)
+    m_own(1)
+    stream(0)
+    m_side(0)
+    a_own(2)
+    a_side(1)
+    a_far(0)
+    m_own(2)
+    stream(1)
+    m_side(1)
+    m_far(0)
+    a_own(3)
+    a_side(2)
+    a_far(1)
+    m_own(3)
+    stream(2)
+    net.exchange_in(cot, k.g, *pair("sem_cot"), loc.at[1], range(S))
+    a_side(3)
+    a_far(2)
+    a_far(3)
+    a_last()
+    rm = [functools.partial(m_side, 2), functools.partial(m_far, 1), functools.partial(m_side, 3), functools.partial(m_far, 2), functools.partial(m_far, 3), m_last]
     own_mask.wait()
     for step in range(1, Z):
         source = lax.rem(net.z + Z - step, Z)
         net.arrived(k.mask.at[pl.ds(source * part, part)], v["sem_mask"].at[1, step])
 
-    def pump(events, n=1):
-        for _ in range(n):
-            if events:
-                events.pop(0)()
-
-    net.exchange_in(cot, k.g, *pair("sem_cot"), loc.at[1], range(S))
     for s in range(S):
         net.exchange_in_done(resid, k.x, v["sem_in"].at[1], loc.at[0], s)
         k.embed(s)
@@ -881,91 +899,101 @@
     pump(rm, len(rm))
     k.up()
     k.down()
-    net.flush()
     for s in range(S):
         net.exchange_out(k.out, resid_out, *pair("sem_out"), loc.at[2], s)
     for s in range(S):
         net.exchange_in_done(cot, k.g, v["sem_cot"].at[1], loc.at[1], s)
     k.mask_cotangent()
     k.grad_pre()
-    k.grad_down()
-    total_m, total_a = k.mid.at[pl.ds(0, sm.shape[0])], k.mid.at[pl.ds(sm.shape[0], sa.shape[0])]
-    m = net.scatter(wm, half, v["inbox"], *pair("sem_rm"), total_m)
-    m["core_send"](2)
-    m["core_send"](3)
-    k.grad_up()
-    m["core_send"](0)
-    m["core_send"](1)
-    m["core_add"](2)
-    m["core_add"](3)
+    net.flush(wm)
+    k.turn_activated()
+    rows = sa.shape[0]
+    parts = sm.shape[0] // rows
+    boxes = v["inbox"].shape[0] // parts
+    totals = [v["total"].at[pl.ds(p * rows, rows)] for p in range(parts + 1)]
+    pieces = [
+        net.scatter(wm, half, p, v["inbox"], p * boxes, v["sem_rm"].at[0, p], v["sem_rm"].at[1, p], totals[p])
+        for p in range(parts)
+    ]
+    (p_core, p_first, p_second, p_own, p_third, p_z, p_zz, p_final) = pieces[0]
+    (q_core, q_first, q_second, q_own, q_third, q_z, q_zz, q_final) = pieces[1]
+    k.grad_down(0, parts)
+    k.grad_up(0, parts)
+    p_core()
+    k.grad_down(1, parts)
+    p_first()
+    k.grad_up(1, parts)
+    q_core()
     k.grad_normed_two()
-    m["core_add"](0)
-    m["core_add"](1)
-    m["first_send"]()
+    q_first()
     k.norm_two_back()
     k.grad_outer()
     k.grad_attended()
-    net.flush()
+    net.flush(resid_out)
     for s in range(S):
         net.exchange_out_done(k.out, resid_out, v["sem_out"].at[1], loc.at[2], s)
     k.attend_back_sequence(0)
-    m["second"]()
+    p_second()
+    k.attend_back_sequence(1)
+    p_own()
+    q_second()
+    k.attend_back_sequence(2)
+    p_third()
+    p_z()
+    k.grad_inner()
+    q_own()
+    q_third()
+    q_z()
+    p_zz()
     k.grad_normed_one(0)
     k.norm_one_back(0)
     net.exchange_out(k.x, grad_in, *pair("sem_gin"), loc.at[3], 0)
-    m["second_own"]()
-    k.attend_back_sequence(1)
+    q_zz()
+    p_final()
+    credit = v["credit"]
+    mesh_id = pl.DeviceIdType.MESH
+    peers = ((net.core, net.z), (net.xn, net.z), (net.yn, net.z), (net.r, net.near), (net.r, net.far))
+    for peer in peers:
+        pl.semaphore_signal(credit, 1, device_id=peer, device_id_type=mesh_id)
     k.grad_normed_one(1)
+    pl.semaphore_wait(credit, len(peers))
+    (a_core, a_first, a_second, a_own, a_third, a_z, a_zz, a_final) = net.scatter(
+        ga, 0, 0, v["inbox"], 0, *pair("sem_ra"), totals[parts]
+    )
+    a_core()
     k.norm_one_back(1)
     net.exchange_out(k.x, grad_in, *pair("sem_gin"), loc.at[3], 1)
-    m["third"]()
-    m["line"](3)
-    k.attend_back_sequence(2)
+    a_first()
     k.grad_normed_one(2)
-    m["line"](2)
     k.norm_one_back(2)
     net.exchange_out(k.x, grad_in, *pair("sem_gin"), loc.at[3], 2)
-    m["line"](1)
-    k.grad_inner()
     for i in range(8):
         v["every"][me, i : i + 1, :] = jnp.sum(k.small[i], axis=0, keepdims=True)
-    re = net.gather(v["every"], *pair("sem_e"))
-    m["final"]()
-    credit = v["credit"]
-    mesh_id = pl.DeviceIdType.MESH
-    for peer in (net.core, net.xn, net.yn):
-        pl.semaphore_signal(credit, 1, device_id=(peer, net.z), device_id_type=mesh_id)
-    pl.when(net.has_right)(
-        lambda: pl.semaphore_signal(credit, 1, device_id=(net.r, net.z + 1), device_id_type=mesh_id)
-    )
-    pl.when(net.has_left)(
-        lambda: pl.semaphore_signal(credit, 1, device_id=(net.r, net.z - 1), device_id_type=mesh_id)
-    )
-    pl.semaphore_wait(credit, 3 + jnp.where(net.has_right, 1, 0) + jnp.where(net.has_left, 1, 0))
-    a = net.scatter(ga, 0, v["inbox"], *pair("sem_ra"), total_a)
-    for c in range(4):
-        a["core_send"](c)
-    pump(re, 2)
-    for c in range(4):
-        a["core_add"](c)
-    a["first_send"]()
+    e_own, e_side, e_far, e_last = net.gather(v["every"], *pair("sem_e"))
+    re = [functools.partial(e_own, 0), functools.partial(e_own, 1)]
+    for i in range(Z):
+        if i + 2 < Z:
+            re.append(functools.partial(e_own, i + 2))
+        re.append(functools.partial(e_side, i))
+        if i:
+            re.append(functools.partial(e_far, i - 1))
+    re += [functools.partial(e_far, Z - 1), e_last]
     pump(re, 4)
-    a["second"]()
-    a["second_own"]()
-    pump(re, 2)
-    a["third"]()
-    for i in (3, 2, 1):
-        a["line"](i)
-        pump(re, 1)
+    q_final()
+    a_second()
+    a_own()
+    pump(re, 3)
+    a_third()
+    a_z()
+    pump(re, 1)
+    a_zz()
     pump(re, len(re))
-    a["final"]()
+    a_final()
     for s in range(S):
         net.exchange_out_done(k.x, grad_in, v["sem_gin"].at[1], loc.at[3], s)
-    outs = [
-        pltpu.make_async_copy(total_m, tm, loc.at[4, 0]),
-        pltpu.make_async_copy(total_a, ta, loc.at[4, 1]),
-        pltpu.make_async_copy(v["every"], every_out, loc.at[4, 2]),
-    ]
+    outs = [pltpu.make_async_copy(totals[parts], ta, loc.at[4, 0])]
+    outs += [pltpu.make_async_copy(totals[p], tm.at[pl.ds(p * rows, rows)], loc.at[0, p]) for p in range(parts)]
+    outs.append(pltpu.make_async_copy(v["every"], every_out, loc.at[4, 2]))
     for copy in outs:
         copy.start()
     for copy in outs:
@@ -1016,7 +1044,7 @@
     scratch = [
         pltpu.VMEM((GROUPS, *sa.shape), BF),
         pltpu.VMEM((GROUPS * 3 // 2, *sm.shape), BF),
-        pltpu.VMEM((4 * Z + 6 * (Z // 2) + 2 * (Z - 1), *sm.shape), BF),
+        pltpu.VMEM((sm.shape[0] // sa.shape[0] * (4 * Z + 6 * (Z // 2) + Z - 1), *sa.shape), BF),
         pltpu.VMEM((T, D), BF),
         pltpu.VMEM((T, D), BF),
         pltpu.VMEM((L, LANES), BF),
@@ -1026,8 +1054,10 @@
         *(dma((2, S * (Z - 1))) for _ in range(4)),
         dma((2, Z)),
         dma((5, S)),
-        *(dma((2, 16)) for _ in range(2)),
+        dma((2, 16)),
+        dma((2, sm.shape[0] // sa.shape[0], 16)),
         pltpu.SemaphoreType.REGULAR,
+        pltpu.VMEM((sa.shape[0] + sm.shape[0], D), F32),
     ]
     resid_out, grad_in, ta, tm, every = pl.pallas_call(
         functools.partial(whole_kernel, (Z, S, part)),

time: 337 us -> 283 us (0.84)
  Pallas kernels: 289 us -> 234 us
    pallas_call x1, Pallas kernels: 289 us -> 234 us  [fast(): pl.pallas_call(functools.partial(whole_kernel, (Z, S, part)), out_shape=(...]
where the time goes in v3:
time: 283 us; the launch traced here: 282 us
  Pallas kernels  234 us (83%)
  local copies, waits for them, and re-layouts  16.2 us (6%)
  other arithmetic  10.8 us (4%)
  matrix products  9.96 us (4%)
  blocking collectives  9.46 us (3%)
    pallas_call x1, Pallas kernels, fast(): pl.pallas_call(functools.partial(whole_kernel, (Z, S, part)), out_shape=(...  234 us
    dot_general x1, matrix products, finish(): jnp.dot(chosen, every[:, :S].reshape(-1, D), precision=lax.Precision.HIGH...  9.96 us
    unnamed x1, blocking collectives  9.46 us
    unnamed x33, local copies, waits for them, and re-layouts  6.28 us

profile of v3, /device:TPU:0, one launch (start us, length us, event | category | flops | bytes accessed | tf_op | source)
XLA Modules:
  0.0 282.2 jit_solution(15283716879548521022)
XLA Ops:
  0.7 1.2 dynamic-slice
  2.6 0.9 dynamic-update-slice
  3.4 9.5 %all-reduce.3 = s32[96]{0:T(128)S(1)} all-reduce(s32[96]{0:T(128)S(1)} %dynamic-update-slice), channel_id=1, replica_groups=mesh['rows'=8,'seq'=4] {'rows'}, use_global_device_ids=true, to_apply=%add.3 | all-reduce | flops 96 | bytes 768
  12.9 0.7 compare_and_fusion
  13.6 0.7 convert_element_type.22
  14.3 2.4 gather_fusion
  16.8 0.1 broadcast_select_fusion.2
  16.9 0.6 pad.13.time
  17.5 1.3 pad.14.norm
  18.8 0.1 copy.32
  19.0 0.7 pad.12.mask_in
  19.6 1.0 convert_element_type.23
  20.6 0.1 reshape.70
  20.7 0.1 reshape.69
  20.8 0.7 bitcast_select_fusion.1.sa
  21.5 1.1 convert_element_type.24
  22.6 0.3 reshape.72
  22.9 0.1 reshape.71
  23.1 0.0 copy-start.10
  23.1 0.0 copy-start.11
  23.1 0.0 copy-start.12
  23.1 0.8 bitcast_select_fusion.sm
  23.9 0.0 copy-start.4
  23.9 0.0 copy-start.8
  23.9 234.2 %shard_map.279 = (bf16[12,64,768]{2,1,0:T(8,128)(2,1)}, bf16[12,64,768]{2,1,0:T(8,128)(2,1)}, f32[96,768]{1,0:T(8,128)}, f32[192,768]{1,0:T(8,128)}, f32[32,8,768]{2,1,0:T(8,128)}) custom-call(bf16[12,64,768]{2,1,0:T(8,128)(2,1)} %resid.1, bf16[12,64,768]{2,1,0:T(8,128)(2,1)} %cot.1, bf16[4,64,128]{2,1,0:T(8,128)(2,1)} %pad.12.mask_in, f32[8,768]{1,0:T(8,128)} %pad.13.time, ...), custom_call_target="tpu_custom_call" | custom-call | tf_op jit(solution)/shard_map/pallas_call | solution.py:1062
  258.0 0.0 copy-start.5
  258.0 1.3 slice_reduce_fusion
  259.3 0.0 copy-start
  259.3 1.2 slice.7
  260.6 0.9 reshape.77
  261.5 0.0 copy-done.10
  261.5 0.0 copy-done.11
  261.5 0.0 copy-done.12
  261.5 0.6 multiply_subtract_fusion.3
  262.1 1.0 reshape.74
  263.1 0.0 copy-done.5
  263.1 0.2 copy.40
  263.3 0.2 reshape.73
  263.5 0.0 copy-done.4
  263.5 0.0 copy-done.8
  263.5 0.0 copy-start.1
  263.5 0.0 copy-start.6
  263.5 2.2 fusion.10
  265.7 0.0 copy-start.7
  265.7 0.0 copy-done
  265.7 0.4 copy.39
  266.1 0.2 reshape.75
  266.4 0.0 copy-done.1
  266.4 0.0 copy-done.6
  266.4 0.4 copy-done.7
  266.8 0.0 copy-start.9
  266.8 0.0 copy-start.13
  266.8 1.7 fusion.8
  268.4 0.0 copy-done.9
  268.4 1.1 copy-done.13
  269.5 0.0 copy-start.3
  269.5 10.0 %multiply_subtract_fusion = (f32[1000,768]{1,0:T(8,128)}, f32[1000,768]{1,0:T(8,128)}, f32[1000,768]{1,0:T(8,128)}) fusion(f32[1000,768]{1,0:T(8,128)S(1)} %copy-done.13, f32[1000,768]{1,0:T(8,128)} %param.30, f32[1000,768]{1,0:T(8,128)} %param.31, f32[96,768]{1,0:T(8,128)S(1)} %copy-done.9, s32[96]{0:T(128)S(1)} %all-reduce.3), kind=kOutput, calls=%fused_computation.4 | convolution fusion | flops 895584000 | bytes 18727296 | tf_op jit(solution)/shard_map/dot_general | solution.py:792
  279.4 0.0 copy-start.2
  279.5 0.0 copy-done.3
  279.5 1.0 copy.44
  280.5 0.7 copy-done.2
  281.1 1.0 copy.45
  (6 shorter events, 0.1 us)
Async XLA Ops:
  23.1 238.4 %copy-start.10 = (f32[5,768]{1,0:T(8,128)S(1)}, f32[5,768]{1,0:T(8,128)}, u32[]{:S(2)}) copy-start(f32[5,768]{1,0:T(8,128)} %param.26) | copy-start | bytes 46084
  23.1 238.4 %copy-start.11 = (f32[5,768]{1,0:T(8,128)S(1)}, f32[5,768]{1,0:T(8,128)}, u32[]{:S(2)}) copy-start(f32[5,768]{1,0:T(8,128)} %param.27) | copy-start | bytes 46084
  23.1 238.4 %copy-start.12 = (f32[5,768]{1,0:T(8,128)S(1)}, f32[5,768]{1,0:T(8,128)}, u32[]{:S(2)}) copy-start(f32[5,768]{1,0:T(8,128)} %param.28) | copy-start | bytes 46084
  23.9 239.6 %copy-start.4 = (f32[73728]{0:T(1024)S(1)}, f32[73728]{0:T(1024)}, u32[]{:S(2)}) copy-start(f32[73728]{0:T(1024)} %param.20) | copy-start | bytes 884740
  23.9 239.6 %copy-start.8 = (f32[73728]{0:T(1024)S(1)}, f32[73728]{0:T(1024)}, u32[]{:S(2)}) copy-start(f32[73728]{0:T(1024)} %param.21) | copy-start | bytes 884740
  258.0 5.1 %copy-start.5 = (f32[96,768]{1,0:T(8,128)S(1)}, f32[96,768]{1,0:T(8,128)}, u32[]{:S(2)}) copy-start(f32[96,768]{1,0:T(8,128)} %get-tuple-element.23) | copy-start | bytes 884740
  259.3 6.4 %copy-start = (f32[192,768]{1,0:T(8,128)S(1)}, f32[192,768]{1,0:T(8,128)}, u32[]{:S(2)}) copy-start(f32[192,768]{1,0:T(8,128)} %get-tuple-element.24) | copy-start | bytes 1769476
  263.5 2.9 %copy-start.1 = (f32[147456]{0:T(1024)S(1)}, f32[147456]{0:T(1024)}, u32[]{:S(2)}) copy-start(f32[147456]{0:T(1024)} %param.23) | copy-start | bytes 1769476
  263.5 2.9 %copy-start.6 = (f32[147456]{0:T(1024)S(1)}, f32[147456]{0:T(1024)}, u32[]{:S(2)}) copy-start(f32[147456]{0:T(1024)} %param.24) | copy-start | bytes 1769476
  265.7 1.1 copy-start.7
  266.8 1.7 copy-start.9
  266.8 2.7 copy-start.13
  269.5 10.0 %copy-start.3 = (bf16[12,64,768]{2,1,0:T(8,128)(2,1)S(1)}, bf16[12,64,768]{2,1,0:T(8,128)(2,1)}, u32[]{:S(2)}) copy-start(bf16[12,64,768]{2,1,0:T(8,128)(2,1)} %get-tuple-element.58) | copy-start | bytes 3538948
  279.4 1.7 copy-start.2

commit v4 on v3

--- a/solution.py
+++ b/solution.py
@@ -76,7 +76,9 @@
         return ref.at[pl.ds(ref.shape[0] // 2 + j * used, used), :, pl.ds(pl.multiple_of(c, n), n)]
 
     def mask_col(self, s, base, n):
-        return self.mask[pl.ds(base, n), s : s + 1].astype(F32)
+        m = self.mask[pl.ds(base, n), :].astype(F32)
+        lane = lax.broadcasted_iota(jnp.int32, m.shape, 1)
+        return jnp.sum(jnp.where(lane == self.lane + s, m, 0.0), axis=-1, keepdims=True)
 
     def embed(self, s):
         def body(i, _):
@@ -285,8 +287,8 @@
             rows = pl.ds(pl.multiple_of(i * ROW_BLOCK, ROW_BLOCK), ROW_BLOCK)
             xhat, rs = norm_stats(self.mid[rows, :])
             dy = self.dn[rows, :]
-            add_small(self.small, 5, dy * xhat)
-            add_small(self.small, 6, dy)
+            add_small(self.small, 2, dy * xhat)
+            add_small(self.small, 3, dy)
             e = dy * self.norm[2:3, :]
             back = (e - jnp.mean(e, -1, keepdims=True) - xhat * jnp.mean(e * xhat, -1, keepdims=True)) * rs
             gm = self.g[rows, :].astype(F32) + back
@@ -372,13 +374,13 @@
             rows = pl.ds(pl.multiple_of(s * self.L + base, ROW_BLOCK), ROW_BLOCK)
             xhat, rs = norm_stats(self.h[rows, :])
             dy = self.mid[rows, :]
-            add_small(self.small, 3, dy * xhat)
-            add_small(self.small, 4, dy)
+            add_small(self.small, 0, dy * xhat)
+            add_small(self.small, 1, dy)
             e = dy * self.norm[0:1, :]
             back = (e - jnp.mean(e, -1, keepdims=True) - xhat * jnp.mean(e * xhat, -1, keepdims=True)) * rs
             gs = self.dn[rows, :] + back
-            add_small(self.small, s, gs)
-            add_small(self.small, 7, gs * self.mask_col(s, base, ROW_BLOCK))
+            add_small(self.small, 5 + s, gs)
+            add_small(self.small, 4, gs * self.mask_col(s, base, ROW_BLOCK))
             self.x[rows, :] = gs.astype(BF)
             return 0
 
@@ -533,6 +535,48 @@
 
         return own, side, far, last
 
+    def gather_small(self, w, ss, rs):
+        Z, z = self.Z, self.z
+        half = Z // 2
+
+        def block(row, lo=0, n=Z):
+            return w.at[pl.ds(row * Z + lo, n)]
+
+        def go(ref, n, peer):
+            self.send(ref, ref, ss.at[n], rs.at[n], peer)
+
+        def along_z():
+            for step in range(1, Z):
+                go(block(self.r, z, 1), step, (self.r, lax.rem(z + step, Z)))
+
+        def spread():
+            for step in range(1, Z):
+                self.arrived(block(self.r, lax.rem(z + Z - step, Z), 1), rs.at[step])
+            go(block(self.r), 4, (self.xn, z))
+            go(block(self.r), 5, (self.yn, z))
+            go(block(self.r), 6, (self.core, z))
+
+        def forward():
+            self.arrived(block(self.xn), rs.at[4])
+            go(block(self.xn, 0, half), 7, (self.yn, z))
+            self.arrived(block(self.yn), rs.at[5])
+            go(block(self.yn, half, half), 8, (self.xn, z))
+            go(block(self.xn), 9, (self.core, z))
+            go(block(self.yn), 10, (self.core, z))
+
+        def corner():
+            self.arrived(block(self.diag, 0, half), rs.at[7])
+            self.arrived(block(self.diag, half, half), rs.at[8])
+            go(block(self.diag), 11, (self.core, z))
+
+        def last():
+            self.arrived(block(self.core), rs.at[6])
+            self.arrived(block(flip(self.xn, 1)), rs.at[9])
+            self.arrived(block(flip(self.yn, 1)), rs.at[10])
+            self.arrived(block(flip(self.diag, 1)), rs.at[11])
+
+        return along_z, spread, forward, corner, last
+
     def exchange_in(self, src, dst, ss, rs, local, seqs):
         L = self.part * self.Z
         for i in seqs:
@@ -669,7 +713,7 @@
     pltpu.sync_copy(x, gin)
     pltpu.sync_copy(g_in, refs["g"])
     layer = Layer(
-        x=gin, mask=mask, time=time, norm=norm, wa=wa, wm=wm, out=out, ga=ga, gm_down=gm, gm_up=gm, small=sums, **refs
+        x=gin, mask=mask, time=time, norm=norm, wa=wa, wm=wm, out=out, ga=ga, gm_down=gm, gm_up=gm, small=sums, lane=0, **refs
     )
     run_all(layer)
     for i in range(8):
@@ -787,9 +831,9 @@
 
 def finish(resid_out, grad_in, steps, every, attn, mlp, norm, time, S):
     D = every.shape[2]
-    norm_grad = jnp.sum(every[:, 3:8], axis=0)
+    norm_grad = jnp.sum(every[:, :5], axis=0)
     chosen = (jnp.arange(time[0].shape[0], dtype=jnp.int32)[:, None] == steps[None, :]).astype(F32)
-    time_grad = jnp.dot(chosen, every[:, :S].reshape(-1, D), precision=lax.Precision.HIGHEST)
+    time_grad = jnp.dot(chosen, every[:, 5 : 5 + S].reshape(-1, D), precision=lax.Precision.HIGHEST)
     return (
         resid_out,
         grad_in,
@@ -806,7 +850,7 @@
 
 
 def whole_kernel(
-    cfg, resid, cot, mask_in, time, norm, sa, sm, resid_out, grad_in, ta, tm, every_out, *scratch
+    cfg, resid, cot, mask_in, time, tags, norm, sa, sm, resid_out, grad_in, ta, tm, every_out, *scratch
 ):
     Z, S, part = cfg
     names = (
@@ -821,7 +865,7 @@
     grads = wm.at[pl.ds(half, GROUPS)]
     k = Layer(
         x=v["x"], out=v["x"], g=v["g"], mask=v["mask"], time=time, norm=norm, wa=v["wa"], wm=wm.at[pl.ds(0, GROUPS)],
-        ga=ga, gm_up=grads, gm_down=grads, small=v["sums"], gb=v["n2"],
+        ga=ga, gm_up=grads, gm_down=grads, small=v["sums"], gb=v["n2"], lane=lax.axis_index("seq") * S,
         **{n: v[n] for n in LAYER_REFS[:-1]},
     )
     net = Links(Z, S, part)
@@ -856,8 +900,8 @@
     for step in range(1, Z):
         to = lax.rem(net.z + step, Z)
         rows = pl.ds(net.z * part, part)
-        net.send(mask_in.at[to], k.mask.at[rows], v["sem_mask"].at[0, step], v["sem_mask"].at[1, step], (net.r, to))
-    own_mask = pltpu.make_async_copy(mask_in.at[net.z], k.mask.at[pl.ds(net.z * part, part)], loc.at[4, 2])
+        net.send(mask_in, k.mask.at[rows], v["sem_mask"].at[0, step], v["sem_mask"].at[1, step], (net.r, to))
+    own_mask = pltpu.make_async_copy(mask_in, k.mask.at[pl.ds(net.z * part, part)], loc.at[4, 2])
     own_mask.start()
     a_own(1)
     a_side(0)
@@ -890,6 +934,7 @@
     for s in range(S):
         net.exchange_in_done(resid, k.x, v["sem_in"].at[1], loc.at[0], s)
         k.embed(s)
+        pump(rm)
         k.project(s)
         pump(rm)
         k.attend_sequence(s)
@@ -925,6 +970,10 @@
     k.grad_up(1, parts)
     q_core()
     k.grad_normed_two()
+    credit = v["credit"]
+    peers = ((net.core, net.z), (net.xn, net.z), (net.yn, net.z), (net.r, net.near), (net.r, net.far))
+    for peer in peers:
+        pl.semaphore_signal(credit, 1, device_id=peer, device_id_type=pl.DeviceIdType.MESH)
     q_first()
     k.norm_two_back()
     k.grad_outer()
@@ -934,60 +983,49 @@
         net.exchange_out_done(k.out, resid_out, v["sem_out"].at[1], loc.at[2], s)
     k.attend_back_sequence(0)
     p_second()
+    k.grad_normed_one(0)
+    k.norm_one_back(0)
+    net.exchange_out(k.x, grad_in, *pair("sem_gin"), loc.at[3], 0)
     k.attend_back_sequence(1)
     p_own()
     q_second()
+    k.grad_normed_one(1)
+    k.norm_one_back(1)
+    net.exchange_out(k.x, grad_in, *pair("sem_gin"), loc.at[3], 1)
     k.attend_back_sequence(2)
     p_third()
     p_z()
     k.grad_inner()
+    pl.semaphore_wait(credit, len(peers))
+    (a_core, a_first, a_second, a_own, a_third, a_z, a_zz, a_final) = net.scatter(
+        ga, 0, 0, wm.reshape(wm.shape[0] * parts, rows, wm.shape[2]), 0, *pair("sem_ra"), totals[parts]
+    )
+    a_core()
+    k.grad_normed_one(2)
+    a_first()
+    k.norm_one_back(2)
+    net.exchange_out(k.x, grad_in, *pair("sem_gin"), loc.at[3], 2)
+    for i in range(8):
+        v["every"][me, i : i + 1, 0 : k.D] = jnp.sum(k.small[i], axis=0, keepdims=True)
+    v["every"][me, :, k.D : k.D + LANES] = tags[...]
+    e_z, e_spread, e_forward, e_corner, e_last = net.gather_small(v["every"], *pair("sem_e"))
+    e_z()
     q_own()
     q_third()
     q_z()
     p_zz()
-    k.grad_normed_one(0)
-    k.norm_one_back(0)
-    net.exchange_out(k.x, grad_in, *pair("sem_gin"), loc.at[3], 0)
+    e_spread()
+    a_second()
     q_zz()
+    e_forward()
+    a_own()
     p_final()
-    credit = v["credit"]
-    mesh_id = pl.DeviceIdType.MESH
-    peers = ((net.core, net.z), (net.xn, net.z), (net.yn, net.z), (net.r, net.near), (net.r, net.far))
-    for peer in peers:
-        pl.semaphore_signal(credit, 1, device_id=peer, device_id_type=mesh_id)
-    k.grad_normed_one(1)
-    pl.semaphore_wait(credit, len(peers))
-    (a_core, a_first, a_second, a_own, a_third, a_z, a_zz, a_final) = net.scatter(
-        ga, 0, 0, v["inbox"], 0, *pair("sem_ra"), totals[parts]
-    )
-    a_core()
-    k.norm_one_back(1)
-    net.exchange_out(k.x, grad_in, *pair("sem_gin"), loc.at[3], 1)
-    a_first()
-    k.grad_normed_one(2)
-    k.norm_one_back(2)
-    net.exchange_out(k.x, grad_in, *pair("sem_gin"), loc.at[3], 2)
-    for i in range(8):
-        v["every"][me, i : i + 1, :] = jnp.sum(k.small[i], axis=0, keepdims=True)
-    e_own, e_side, e_far, e_last = net.gather(v["every"], *pair("sem_e"))
-    re = [functools.partial(e_own, 0), functools.partial(e_own, 1)]
-    for i in range(Z):
-        if i + 2 < Z:
-            re.append(functools.partial(e_own, i + 2))
-        re.append(functools.partial(e_side, i))
-        if i:
-            re.append(functools.partial(e_far, i - 1))
-    re += [functools.partial(e_far, Z - 1), e_last]
-    pump(re, 4)
-    q_final()
-    a_second()
-    a_own()
-    pump(re, 3)
+    e_corner()
     a_third()
     a_z()
-    pump(re, 1)
+    q_final()
     a_zz()
-    pump(re, len(re))
+    e_last()
     a_final()
     for s in range(S):
         net.exchange_out_done(k.x, grad_in, v["sem_gin"].at[1], loc.at[3], s)
@@ -999,6 +1037,117 @@
     for copy in outs:
         copy.wait()
     net.flush()
+
+
+def walk(is_split, parts, rows, D, visit):
+    per = D // LANES
+
+    def split():
+        n = rows // parts
+        for j in range(parts):
+            for c in range(per):
+                visit(pl.ds(j * n, n), pl.ds(c * LANES, LANES), pl.ds(j * per + c, n, stride=parts * per))
+
+    def plain():
+        for c in range(per):
+            visit(pl.ds(0, rows), pl.ds(c * LANES, LANES), pl.ds(c, rows, stride=per))
+
+    pl.when(is_split)(split)
+    pl.when(jnp.logical_not(is_split))(plain)
+
+
+def device_kinds():
+    Z, R = lax.axis_size("seq"), lax.axis_size("rows")
+    device = lax.axis_index("rows") * Z + lax.axis_index("seq")
+    return device < R * Z * 3 // 4, device < R * Z // 2
+
+
+def before_kernel(S, steps, mask, time_master, attn, mlp, sa, sm, mask_out, time_rows, tags, board, sems):
+    D = sa.shape[1]
+    first = lax.axis_index("seq") * S
+    time_rows[...] = jnp.zeros(time_rows.shape, F32)
+    copies = [
+        pltpu.make_async_copy(time_master.at[pl.ds(steps[first + s], 1)], time_rows.at[pl.ds(s, 1)], sems.at[s])
+        for s in range(S)
+    ]
+    for copy in copies:
+        copy.start()
+    row = lax.broadcasted_iota(jnp.int32, tags.shape, 0)
+    value = jnp.full(tags.shape, -1, jnp.int32)
+    for s in range(S):
+        value = jnp.where(row == 5 + s, steps[first + s], value)
+    tags[...] = value.astype(F32)
+    board[...] = jnp.zeros(board.shape, F32)
+    board[0 : mask.shape[0], 0 : mask.shape[1]] = mask[...].astype(F32)
+    mask_out[...] = board[...].T[0 : mask.shape[1], :].astype(BF)
+    is_inner, is_up = device_kinds()
+
+    def cast(src, dst):
+        def visit(rows, cols, lines):
+            dst[rows, cols] = src[lines, :].astype(BF)
+
+        return visit
+
+    walk(is_inner, 3, sa.shape[0], D, cast(attn, sa))
+    walk(is_up, FF // D, sm.shape[0], D, cast(mlp, sm))
+    for copy in copies:
+        copy.wait()
+
+
+def adamw_low(master, moment_one, moment_two, gradient, step_rate):
+    first_new = 0.5 * moment_one + 0.5 * gradient
+    second_new = 0.5 * moment_two + 0.5 * gradient * gradient
+    scale = 1.0 / (1.0 - 0.5**STEP)
+    update = (first_new * scale) / (jnp.sqrt(second_new * scale) + 1e-08)
+    return master - step_rate * (update + 0.1 * master), first_new, second_new
+
+
+def after_kernel(ta, tm, every, *refs):
+    D = ta.shape[1]
+    attn, mlp, norm, time = refs[0:3], refs[3:6], refs[6:9], refs[9:12]
+    attn_out, mlp_out, norm_out, time_out = refs[12:16], refs[16:20], refs[20:23], refs[23:26]
+    step = pl.program_id(0)
+    is_inner, is_up = device_kinds()
+
+    def update(olds, news, grad, rate):
+        def visit(rows, cols, lines):
+            values = adamw_low(*(old[lines, :] for old in olds), grad[rows, cols], rate)
+            for new, value in zip(news, values):
+                new[lines, :] = value
+
+        return visit
+
+    @pl.when(step == 0)
+    def _():
+        walk(is_inner, 3, ta.shape[0], D, update(attn, attn_out[:3], ta, 0.05))
+        attn_out[3][...] = attn_out[0][...].astype(BF)
+        total = every[0, :, 0:D]
+        for i in range(1, every.shape[0]):
+            total = total + every[i, :, 0:D]
+        values = adamw_low(*(old[...] for old in norm), total[0:5], 0.2)
+        for new, value in zip(norm_out, values):
+            new[...] = value
+
+    @pl.when(step == 1)
+    def _():
+        walk(is_up, FF // D, tm.shape[0], D, update(mlp, mlp_out[:3], tm, 0.03))
+        mlp_out[3][...] = mlp_out[0][...].astype(BF)
+
+    n = time[0].shape[0]
+    rows = every.shape[0] * every.shape[1]
+    tag = every[:, :, D : D + LANES].reshape(rows, LANES)[:, 0:1]
+    at = (lax.broadcasted_iota(jnp.int32, (rows, n), 1) + step * n).astype(F32)
+    chosen = jnp.where(tag == at, 1.0, 0.0).astype(BF)
+    rest = every[:, :, 0:D].reshape(rows, D)
+    grad = None
+    for _ in range(3):
+        low = rest.astype(BF)
+        rest = rest - low.astype(F32)
+        y = dot(chosen, low, TN)
+        grad = y if grad is None else grad + y
+    values = adamw_low(*(old[...] for old in time), grad, 0.3)
+    for new, value in zip(time_out, values):
+        new[...] = value
 
 
 def fast(
@@ -1026,21 +1175,29 @@
     part = resid_in.shape[1]
     L = part * Z
     T = S * L
-    device = lax.axis_index("rows") * Z + lax.axis_index("seq")
-    attn_low, mlp_low = attn_master.astype(BF), mlp_master.astype(BF)
-    inner_shards = R * Z * 3 // 4
-    is_inner, is_up = device < inner_shards, device < R * Z // 2
-    sa = jnp.where(is_inner, rows_split(attn_low, 1, 3, D)[0], attn_low.reshape(-1, D))
-    sm = jnp.where(is_up, rows_split(mlp_low, 1, FF // D, D)[0], mlp_low.reshape(-1, D))
-    mask_in = mask.astype(BF).reshape(Z, S, part).transpose(0, 2, 1)
-    mask_in = jnp.pad(mask_in, ((0, 0), (0, 0), (0, LANES - S)))
-    steps_use = lax.dynamic_slice_in_dim(steps_row, lax.axis_index("seq") * S, S, 0)
-    time_rows = pad_rows(jnp.take(time_master, steps_use, axis=0))
     V = pl.BlockSpec(memory_space=pltpu.VMEM)
     A = pl.BlockSpec(memory_space=pl.ANY)
     shape = jax.ShapeDtypeStruct
+    dma = pltpu.SemaphoreType.DMA
+    attn = [a.reshape(-1, LANES) for a in (attn_master, attn_first, attn_second)]
+    mlp = [a.reshape(-1, LANES) for a in (mlp_master, mlp_first, mlp_second)]
+    sa_shape = (attn_master.shape[0] // D, D)
+    sm_shape = (mlp_master.shape[0] // D, D)
+    sa, sm, mask_in, time_rows, tags = pl.pallas_call(
+        functools.partial(before_kernel, S),
+        out_shape=(
+            shape(sa_shape, BF),
+            shape(sm_shape, BF),
+            shape((part, LANES), BF),
+            shape((8, D), F32),
+            shape((8, LANES), F32),
+        ),
+        in_specs=[pl.BlockSpec(memory_space=pltpu.SMEM), V, A, V, V],
+        out_specs=(V,) * 5,
+        scratch_shapes=[pltpu.VMEM((LANES, LANES), F32), dma((S,))],
+        compiler_params=pltpu.CompilerParams(vmem_limit_bytes=63 << 20),
+    )(steps_row, mask, time_master, attn[0], mlp[0])
     sc = layer_scratch(T, D, S, L)
-    dma = pltpu.SemaphoreType.DMA
     scratch = [
         pltpu.VMEM((GROUPS, *sa.shape), BF),
         pltpu.VMEM((GROUPS * 3 // 2, *sm.shape), BF),
@@ -1049,8 +1206,8 @@
         pltpu.VMEM((T, D), BF),
         pltpu.VMEM((L, LANES), BF),
         *(sc[n] for n in LAYER_REFS),
-        pltpu.VMEM((R * Z, 8, D), F32),
-        *(dma((2, 40)) for _ in range(3)),
+        pltpu.VMEM((R * Z, 8, D + LANES), F32),
+        *(dma((2, n)) for n in (40, 40, 12)),
         *(dma((2, S * (Z - 1))) for _ in range(4)),
         dma((2, Z)),
         dma((5, S)),
@@ -1066,28 +1223,36 @@
             shape(resid_in.shape, BF),
             shape(sa.shape, F32),
             shape(sm.shape, F32),
-            shape((R * Z, 8, D), F32),
+            shape((R * Z, 8, D + LANES), F32),
         ),
-        in_specs=[A, A, A, V, V, A, A],
+        in_specs=[A, A, A, V, V, V, A, A],
         out_specs=(A,) * 5,
         scratch_shapes=scratch,
         compiler_params=pltpu.CompilerParams(
             collective_id=0, has_side_effects=True, vmem_limit_bytes=63 << 20
         ),
-    )(resid_in, cotangent, mask_in, time_rows, pad_rows(norm_master), sa, sm)
-    attn_grad = jnp.where(is_inner, rows_join(ta[None], 3, D), ta.reshape(-1))
-    mlp_grad = jnp.where(is_up, rows_join(tm[None], FF // D, D), tm.reshape(-1))
-    return finish(
-        resid_out,
-        grad_in,
-        lax.all_gather(steps_row, "rows", axis=0, tiled=True),
-        every,
-        adamw(attn_master, attn_first, attn_second, attn_grad, 0.05),
-        adamw(mlp_master, mlp_first, mlp_second, mlp_grad, 0.03),
-        (norm_master, norm_first, norm_second),
-        (time_master, time_first, time_second),
-        S,
-    )
+    )(resid_in, cotangent, mask_in, time_rows, tags, norm_master, sa, sm)
+    steps = 5
+    norm = (norm_master, norm_first, norm_second)
+    time = (time_master, time_first, time_second)
+    rows = time_master.shape[0] // steps
+    moving = pl.BlockSpec((rows, D), lambda i: (i, 0))
+
+    def fixed(a):
+        return pl.BlockSpec(a.shape, lambda i: (0,) * len(a.shape))
+
+    outs = [shape(a.shape, F32) for a in attn] + [shape(attn[0].shape, BF)]
+    outs += [shape(a.shape, F32) for a in mlp] + [shape(mlp[0].shape, BF)]
+    outs += [shape(a.shape, F32) for a in norm]
+    news = pl.pallas_call(
+        after_kernel,
+        grid=(steps,),
+        out_shape=(*outs, *(shape(a.shape, F32) for a in time)),
+        in_specs=[fixed(a) for a in (ta, tm, every, *attn, *mlp, *norm)] + [moving] * 3,
+        out_specs=(*(fixed(a) for a in outs), *(moving,) * 3),
+        compiler_params=pltpu.CompilerParams(vmem_limit_bytes=63 << 20),
+    )(ta, tm, every, *attn, *mlp, *norm, *time)
+    return (resid_out, grad_in, *(a.reshape(-1) for a in news[:8]), *news[8:])
 
 
 def solution(mesh):

time: 283 us -> 241 us (0.85)
  local copies, waits for them, and re-layouts: 16.2 us -> 3.47 us
  other arithmetic: 10.8 us -> 0 us
  matrix products: 9.96 us -> 0 us
  blocking collectives: 9.46 us -> 0 us
  Pallas kernels: 234 us -> 237 us
    pallas_call x0 -> x2, Pallas kernels: none -> 14.7 us  [the longest x1 12 us: fast(): pl.pallas_call(after_kernel, grid=(steps,), out_shape=(*outs, *(shape(a.s...]
    pallas_call x1, Pallas kernels: 234 us -> 222 us  [fast(): pl.pallas_call(functools.partial(whole_kernel, (Z, S, part)), out_shape=(...]
    dot_general x1 -> x0, matrix products: 9.96 us -> none  [finish(): jnp.dot(chosen, every[:, :S].reshape(-1, D), precision=lax.Precision.HIGH...]
    unnamed x1 -> x0, blocking collectives: 9.46 us -> none
    convert_element_type x5 -> x0, other arithmetic: 6.61 us -> none  [the longest x1 2.18 us: finish(): attn[0].astype(BF)]
    reshape x11 -> x0, local copies, waits for them, and re-layouts: 3.03 us -> none  [the longest x1 0.98 us: fast(): attn_grad = jnp.where(is_inner, rows_join(ta[None], 3, D), ta.reshape(-1))]
    unnamed x33 -> x4, local copies, waits for them, and re-layouts: 6.28 us -> 3.47 us
where the time goes in v4:
time: 241 us
  Pallas kernels  237 us (98%)
  local copies, waits for them, and re-layouts  3.47 us (1%)
    pallas_call x1, Pallas kernels, fast(): pl.pallas_call(functools.partial(whole_kernel, (Z, S, part)), out_shape=(...  222 us
    pallas_call x1, Pallas kernels, fast(): pl.pallas_call(after_kernel, grid=(steps,), out_shape=(*outs, *(shape(a.s...  12 us

profile of v4, /device:TPU:0, one launch (start us, length us, event | category | flops | bytes accessed | tf_op | source)
XLA Modules:
  0.0 240.9 jit_solution(11225967464800994407)
XLA Ops:
  0.6 2.7 %shard_map.279 = (bf16[96,768]{1,0:T(8,128)(2,1)}, bf16[192,768]{1,0:T(8,128)(2,1)}, bf16[64,128]{1,0:T(8,128)(2,1)}, f32[8,768]{1,0:T(8,128)}, f32[8,128]{1,0:T(8,128)}) custom-call(s32[12]{0:T(128)} %steps.1, s32[12,64]{1,0:T(8,128)} %mask.1, f32[1000,768]{1,0:T(8,128)} %refs_9_.1, f32[576,128]{1,0:T(8,128)} %bitcast.16, f32[1152,128]{1,0:T(8,128)} %bitcast.14), custom_call_target="tpu_custom_call" | custom-call | tf_op jit(solution)/shard_map/pallas_call | solution.py:1186
  3.4 222.1 %shard_map.280 = (bf16[12,64,768]{2,1,0:T(8,128)(2,1)}, bf16[12,64,768]{2,1,0:T(8,128)(2,1)}, f32[96,768]{1,0:T(8,128)}, f32[192,768]{1,0:T(8,128)}, f32[32,8,896]{2,1,0:T(8,128)}) custom-call(bf16[12,64,768]{2,1,0:T(8,128)(2,1)} %resid.1, bf16[12,64,768]{2,1,0:T(8,128)(2,1)} %cot.1, bf16[64,128]{1,0:T(8,128)(2,1)} %get-tuple-element.40.mask_in, ...), custom_call_target="tpu_custom_call" | custom-call | tf_op jit(solution)/shard_map/pallas_call | solution.py:1219
  225.4 12.0 %shard_map.281 = (f32[576,128]{1,0:T(8,128)}, f32[576,128]{1,0:T(8,128)}, f32[576,128]{1,0:T(8,128)}, bf16[576,128]{1,0:T(8,128)(2,1)}, f32[1152,128]{1,0:T(8,12...) custom-call(f32[96,768]{1,0:T(8,128)} %get-tuple-element.47.ta, ...), custom_call_target="tpu_custom_call" | custom-call | tf_op jit(solution)/shard_map/pallas_call | solution.py:1247
  237.4 0.0 copy-start
  237.4 2.5 %copy.34 = bf16[12,64,768]{2,1,0:T(8,128)(2,1)} copy(bf16[12,64,768]{2,1,0:T(8,128)(2,1)} %get-tuple-element.80) | data formatting | bytes 2359296
  239.9 0.0 copy-done
  239.9 1.0 copy.35
Async XLA Ops:
  237.4 2.5 %copy-start = (bf16[12,64,768]{2,1,0:T(8,128)(2,1)S(1)}, bf16[12,64,768]{2,1,0:T(8,128)(2,1)}, u32[]{:S(2)}) copy-start(bf16[12,64,768]{2,1,0:T(8,128)(2,1)} %get-tuple-element.81) | copy-start | bytes 3538948

commit v5 on v4

--- a/solution.py
+++ b/solution.py
@@ -517,10 +517,12 @@
         def side(i):
             zz = self.order[i]
             got(self.xn, zz)
-            go(self.xn, zz, (self.yn, z), zz < Z // 2)
+            if i % 2 == 0:
+                go(self.xn, zz, (self.yn, z))
+            go(self.xn, zz, (self.core, z))
             got(self.yn, zz)
-            go(self.yn, zz, (self.xn, z), zz >= Z // 2)
-            go(self.xn, zz, (self.core, z))
+            if i % 2 == 1:
+                go(self.yn, zz, (self.xn, z))
             go(self.yn, zz, (self.core, z))
 
         def far(i):
@@ -905,27 +907,34 @@
     own_mask.start()
     a_own(1)
     a_side(0)
-    m_own(1)
+    a_own(2)
     stream(0)
-    m_side(0)
-    a_own(2)
     a_side(1)
     a_far(0)
-    m_own(2)
-    stream(1)
-    m_side(1)
-    m_far(0)
+    m_own(1)
     a_own(3)
     a_side(2)
     a_far(1)
-    m_own(3)
-    stream(2)
-    net.exchange_in(cot, k.g, *pair("sem_cot"), loc.at[1], range(S))
+    m_side(0)
+    m_own(2)
+    stream(1)
     a_side(3)
     a_far(2)
+    stream(2)
     a_far(3)
     a_last()
-    rm = [functools.partial(m_side, 2), functools.partial(m_far, 1), functools.partial(m_side, 3), functools.partial(m_far, 2), functools.partial(m_far, 3), m_last]
+    net.exchange_in(cot, k.g, *pair("sem_cot"), loc.at[1], range(S))
+    rm = [
+        functools.partial(m_side, 1),
+        functools.partial(m_own, 3),
+        functools.partial(m_far, 0),
+        functools.partial(m_side, 2),
+        functools.partial(m_far, 1),
+        functools.partial(m_side, 3),
+        functools.partial(m_far, 2),
+        functools.partial(m_far, 3),
+        m_last,
+    ]
     own_mask.wait()
     for step in range(1, Z):
         source = lax.rem(net.z + Z - step, Z)

time: 241 us -> 218 us (0.905)
  Pallas kernels: 237 us -> 213 us
    pallas_call x1, Pallas kernels: 222 us -> 199 us  [fast(): pl.pallas_call(functools.partial(whole_kernel, (Z, S, part)), out_shape=(...]
where the time goes in v5:
time: 218 us; the launch traced here: 217 us
  Pallas kernels  213 us (98%)
  local copies, waits for them, and re-layouts  3.47 us (2%)
    pallas_call x1, Pallas kernels, fast(): pl.pallas_call(functools.partial(whole_kernel, (Z, S, part)), out_shape=(...  199 us
    pallas_call x1, Pallas kernels, fast(): pl.pallas_call(after_kernel, grid=(steps,), out_shape=(*outs, *(shape(a.s...  12 us

profile of v5, /device:TPU:0, one launch (start us, length us, event | category | flops | bytes accessed | tf_op | source)
XLA Modules:
  0.0 217.4 jit_solution(2776057095542063008)
XLA Ops:
  0.6 2.7 %shard_map.279 = (bf16[96,768]{1,0:T(8,128)(2,1)}, bf16[192,768]{1,0:T(8,128)(2,1)}, bf16[64,128]{1,0:T(8,128)(2,1)}, f32[8,768]{1,0:T(8,128)}, f32[8,128]{1,0:T(8,128)}) custom-call(s32[12]{0:T(128)} %steps.1, s32[12,64]{1,0:T(8,128)} %mask.1, f32[1000,768]{1,0:T(8,128)} %refs_9_.1, f32[576,128]{1,0:T(8,128)} %bitcast.16, f32[1152,128]{1,0:T(8,128)} %bitcast.14), custom_call_target="tpu_custom_call" | custom-call | tf_op jit(solution)/shard_map/pallas_call | solution.py:1195
  3.4 198.5 %shard_map.280 = (bf16[12,64,768]{2,1,0:T(8,128)(2,1)}, bf16[12,64,768]{2,1,0:T(8,128)(2,1)}, f32[96,768]{1,0:T(8,128)}, f32[192,768]{1,0:T(8,128)}, f32[32,8,896]{2,1,0:T(8,128)}) custom-call(bf16[12,64,768]{2,1,0:T(8,128)(2,1)} %resid.1, bf16[12,64,768]{2,1,0:T(8,128)(2,1)} %cot.1, bf16[64,128]{1,0:T(8,128)(2,1)} %get-tuple-element.40.mask_in, ...), custom_call_target="tpu_custom_call" | custom-call | tf_op jit(solution)/shard_map/pallas_call | solution.py:1228
  201.9 12.0 %shard_map.281 = (f32[576,128]{1,0:T(8,128)}, f32[576,128]{1,0:T(8,128)}, f32[576,128]{1,0:T(8,128)}, bf16[576,128]{1,0:T(8,128)(2,1)}, f32[1152,128]{1,0:T(8,12...) custom-call(f32[96,768]{1,0:T(8,128)} %get-tuple-element.47.ta, ...), custom_call_target="tpu_custom_call" | custom-call | tf_op jit(solution)/shard_map/pallas_call | solution.py:1256
  213.9 0.0 copy-start
  213.9 2.5 %copy.34 = bf16[12,64,768]{2,1,0:T(8,128)(2,1)} copy(bf16[12,64,768]{2,1,0:T(8,128)(2,1)} %get-tuple-element.80) | data formatting | bytes 2359296
  216.3 0.0 copy-done
  216.3 1.0 copy.35
Async XLA Ops:
  213.9 2.5 %copy-start = (bf16[12,64,768]{2,1,0:T(8,128)(2,1)S(1)}, bf16[12,64,768]{2,1,0:T(8,128)(2,1)}, u32[]{:S(2)}) copy-start(bf16[12,64,768]{2,1,0:T(8,128)(2,1)} %get-tuple-element.81) | copy-start | bytes 3538948

commit v6 on v5

--- a/solution.py
+++ b/solution.py
@@ -1113,23 +1113,30 @@
 
 def after_kernel(ta, tm, every, *refs):
     D = ta.shape[1]
-    attn, mlp, norm, time = refs[0:3], refs[3:6], refs[6:9], refs[9:12]
-    attn_out, mlp_out, norm_out, time_out = refs[12:16], refs[16:20], refs[20:23], refs[23:26]
+    flat, norm, time, tokens = refs[0:6], refs[6:9], refs[9:12], refs[12:14]
+    flat_out, norm_out, time_out, tokens_out = refs[14:22], refs[22:25], refs[25:28], refs[28:30]
+    held, low, sems = refs[30:36], refs[36:38], refs[38]
     step = pl.program_id(0)
     is_inner, is_up = device_kinds()
-
-    def update(olds, news, grad, rate):
+    loads = [pltpu.make_async_copy(a, b, sems.at[i]) for i, (a, b) in enumerate(zip(flat, held))]
+    ready = (*held[:3], low[0], *held[3:], low[1])
+    stores = [pltpu.make_async_copy(a, b, sems.at[6 + i]) for i, (a, b) in enumerate(zip(ready, flat_out))]
+
+    def update(kept, grad, rate):
         def visit(rows, cols, lines):
-            values = adamw_low(*(old[lines, :] for old in olds), grad[rows, cols], rate)
-            for new, value in zip(news, values):
+            values = adamw_low(*(old[lines, :] for old in kept), grad[rows, cols], rate)
+            for new, value in zip(kept, values):
                 new[lines, :] = value
 
         return visit
+
+    for new, old in zip(tokens_out, tokens):
+        new[...] = old[...]
 
     @pl.when(step == 0)
     def _():
-        walk(is_inner, 3, ta.shape[0], D, update(attn, attn_out[:3], ta, 0.05))
-        attn_out[3][...] = attn_out[0][...].astype(BF)
+        for copy in loads:
+            copy.start()
         total = every[0, :, 0:D]
         for i in range(1, every.shape[0]):
             total = total + every[i, :, 0:D]
@@ -1139,8 +1146,19 @@
 
     @pl.when(step == 1)
     def _():
-        walk(is_up, FF // D, tm.shape[0], D, update(mlp, mlp_out[:3], tm, 0.03))
-        mlp_out[3][...] = mlp_out[0][...].astype(BF)
+        for copy in loads:
+            copy.wait()
+        walk(is_inner, 3, ta.shape[0], D, update(held[:3], ta, 0.05))
+        low[0][...] = held[0][...].astype(BF)
+        walk(is_up, FF // D, tm.shape[0], D, update(held[3:], tm, 0.03))
+        low[1][...] = held[3][...].astype(BF)
+        for copy in stores:
+            copy.start()
+
+    @pl.when(step == pl.num_programs(0) - 1)
+    def _():
+        for copy in stores:
+            copy.wait()
 
     n = time[0].shape[0]
     rows = every.shape[0] * every.shape[1]
@@ -1250,18 +1268,25 @@
     def fixed(a):
         return pl.BlockSpec(a.shape, lambda i: (0,) * len(a.shape))
 
+    blocks = resid_in.shape[0] // S
+    tokens = pl.BlockSpec((S, part, D), lambda i: (jnp.minimum(i, blocks - 1), 0, 0))
     outs = [shape(a.shape, F32) for a in attn] + [shape(attn[0].shape, BF)]
     outs += [shape(a.shape, F32) for a in mlp] + [shape(mlp[0].shape, BF)]
-    outs += [shape(a.shape, F32) for a in norm]
     news = pl.pallas_call(
         after_kernel,
         grid=(steps,),
-        out_shape=(*outs, *(shape(a.shape, F32) for a in time)),
-        in_specs=[fixed(a) for a in (ta, tm, every, *attn, *mlp, *norm)] + [moving] * 3,
-        out_specs=(*(fixed(a) for a in outs), *(moving,) * 3),
+        out_shape=(*outs, *(shape(a.shape, F32) for a in (*norm, *time)), *(shape(resid_in.shape, BF),) * 2),
+        in_specs=[fixed(a) for a in (ta, tm, every)] + [A] * 6 + [fixed(a) for a in norm] + [moving] * 3 + [tokens] * 2,
+        out_specs=(*(A,) * 8, *(fixed(a) for a in norm), *(moving,) * 3, tokens, tokens),
+        scratch_shapes=[
+            *(pltpu.VMEM(a.shape, F32) for a in (*attn, *mlp)),
+            pltpu.VMEM(attn[0].shape, BF),
+            pltpu.VMEM(mlp[0].shape, BF),
+            dma((14,)),
+        ],
         compiler_params=pltpu.CompilerParams(vmem_limit_bytes=63 << 20),
-    )(ta, tm, every, *attn, *mlp, *norm, *time)
-    return (resid_out, grad_in, *(a.reshape(-1) for a in news[:8]), *news[8:])
+    )(ta, tm, every, *attn, *mlp, *norm, *time, resid_out, grad_in)
+    return (*news[14:], *(a.reshape(-1) for a in news[:8]), *news[8:14])
 
 
 def solution(mesh):

time: 218 us -> 216 us (level)
  local copies, waits for them, and re-layouts: 3.47 us -> 0 us
    unnamed x4 -> x0, local copies, waits for them, and re-layouts: 3.47 us -> none
where the time goes in v6:
time: 216 us; the launch traced here: 215 us
  Pallas kernels  214 us (99%)
    pallas_call x1, Pallas kernels, fast(): pl.pallas_call(functools.partial(whole_kernel, (Z, S, part)), out_shape=(...  199 us
    pallas_call x1, Pallas kernels, fast(): pl.pallas_call(after_kernel, grid=(steps,), out_shape=(*outs, *(shape(a.s...  13.2 us

profile of v6, /device:TPU:0, one launch (start us, length us, event | category | flops | bytes accessed | tf_op | source)
XLA Modules:
  0.0 215.3 jit_solution(7424357284836855440)
XLA Ops:
  0.6 2.7 %shard_map.279 = (bf16[96,768]{1,0:T(8,128)(2,1)}, bf16[192,768]{1,0:T(8,128)(2,1)}, bf16[64,128]{1,0:T(8,128)(2,1)}, f32[8,768]{1,0:T(8,128)}, f32[8,128]{1,0:T(8,128)}) custom-call(s32[12]{0:T(128)} %steps.1, s32[12,64]{1,0:T(8,128)} %mask.1, f32[1000,768]{1,0:T(8,128)} %refs_9_.1, f32[576,128]{1,0:T(8,128)} %bitcast.16, f32[1152,128]{1,0:T(8,128)} %bitcast.14), custom_call_target="tpu_custom_call" | custom-call | tf_op jit(solution)/shard_map/pallas_call | solution.py:1213
  3.4 198.5 %shard_map.280 = (bf16[12,64,768]{2,1,0:T(8,128)(2,1)}, bf16[12,64,768]{2,1,0:T(8,128)(2,1)}, f32[96,768]{1,0:T(8,128)}, f32[192,768]{1,0:T(8,128)}, f32[32,8,896]{2,1,0:T(8,128)}) custom-call(bf16[12,64,768]{2,1,0:T(8,128)(2,1)} %resid.1, bf16[12,64,768]{2,1,0:T(8,128)(2,1)} %cot.1, bf16[64,128]{1,0:T(8,128)(2,1)} %get-tuple-element.42.mask_in, ...), custom_call_target="tpu_custom_call" | custom-call | tf_op jit(solution)/shard_map/pallas_call | solution.py:1246
  201.9 13.2 %shard_map.281 = (f32[576,128]{1,0:T(8,128)}, f32[576,128]{1,0:T(8,128)}, f32[576,128]{1,0:T(8,128)}, bf16[576,128]{1,0:T(8,128)(2,1)}, f32[1152,128]{1,0:T(8,12...) custom-call(f32[96,768]{1,0:T(8,128)} %get-tuple-element.47.ta, ...), custom_call_target="tpu_custom_call" | custom-call | tf_op jit(solution)/shard_map/pallas_call | solution.py:1275

commit v7 on v6

--- a/solution.py
+++ b/solution.py
@@ -1002,14 +1002,14 @@
     k.norm_one_back(1)
     net.exchange_out(k.x, grad_in, *pair("sem_gin"), loc.at[3], 1)
     k.attend_back_sequence(2)
-    p_third()
-    p_z()
     k.grad_inner()
     pl.semaphore_wait(credit, len(peers))
     (a_core, a_first, a_second, a_own, a_third, a_z, a_zz, a_final) = net.scatter(
         ga, 0, 0, wm.reshape(wm.shape[0] * parts, rows, wm.shape[2]), 0, *pair("sem_ra"), totals[parts]
     )
     a_core()
+    p_third()
+    p_z()
     k.grad_normed_one(2)
     a_first()
     k.norm_one_back(2)
@@ -1023,8 +1023,8 @@
     q_third()
     q_z()
     p_zz()
+    a_second()
     e_spread()
-    a_second()
     q_zz()
     e_forward()
     a_own()

time: 216 us -> 215 us (level)
  no operation moved by 1% of the time
where the time goes in v7:
time: 215 us; the launch traced here: 214 us
  Pallas kernels  213 us (99%)
    pallas_call x1, Pallas kernels, fast(): pl.pallas_call(functools.partial(whole_kernel, (Z, S, part)), out_shape=(...  197 us
    pallas_call x1, Pallas kernels, fast(): pl.pallas_call(after_kernel, grid=(steps,), out_shape=(*outs, *(shape(a.s...  13.2 us

profile of v7, /device:TPU:0, one launch (start us, length us, event | category | flops | bytes accessed | tf_op | source)
XLA Modules:
  0.0 213.7 jit_solution(14449563092594351822)
XLA Ops:
  0.6 2.7 %shard_map.279 = (bf16[96,768]{1,0:T(8,128)(2,1)}, bf16[192,768]{1,0:T(8,128)(2,1)}, bf16[64,128]{1,0:T(8,128)(2,1)}, f32[8,768]{1,0:T(8,128)}, f32[8,128]{1,0:T(8,128)}) custom-call(s32[12]{0:T(128)} %steps.1, s32[12,64]{1,0:T(8,128)} %mask.1, f32[1000,768]{1,0:T(8,128)} %refs_9_.1, f32[576,128]{1,0:T(8,128)} %bitcast.16, f32[1152,128]{1,0:T(8,128)} %bitcast.14), custom_call_target="tpu_custom_call" | custom-call | tf_op jit(solution)/shard_map/pallas_call | solution.py:1213
  3.4 196.9 %shard_map.280 = (bf16[12,64,768]{2,1,0:T(8,128)(2,1)}, bf16[12,64,768]{2,1,0:T(8,128)(2,1)}, f32[96,768]{1,0:T(8,128)}, f32[192,768]{1,0:T(8,128)}, f32[32,8,896]{2,1,0:T(8,128)}) custom-call(bf16[12,64,768]{2,1,0:T(8,128)(2,1)} %resid.1, bf16[12,64,768]{2,1,0:T(8,128)(2,1)} %cot.1, bf16[64,128]{1,0:T(8,128)(2,1)} %get-tuple-element.42.mask_in, ...), custom_call_target="tpu_custom_call" | custom-call | tf_op jit(solution)/shard_map/pallas_call | solution.py:1246
  200.3 13.2 %shard_map.281 = (f32[576,128]{1,0:T(8,128)}, f32[576,128]{1,0:T(8,128)}, f32[576,128]{1,0:T(8,128)}, bf16[576,128]{1,0:T(8,128)(2,1)}, f32[1152,128]{1,0:T(8,12...) custom-call(f32[96,768]{1,0:T(8,128)} %get-tuple-element.47.ta, ...), custom_call_target="tpu_custom_call" | custom-call | tf_op jit(solution)/shard_map/pallas_call | solution.py:1275
